TPU v7x, 256 devices: a whole 4x4x8 slice. The times are simulated.
256 devices in a mesh: section: 8 (over z_hi, core), expert: 32 (over x, y, z_lo).
Axes of the slice: x: 4, y: 4, z: 8 (z_hi: 4, z_lo: 2; z = z_hi * 2 + z_lo), core: 2. Of those that a mesh axis runs over, the one named last changes fastest.
Arguments:
- layer_in: bfloat16 [8, 4096, 5120], P('section', 'expert'), may hold values from -50 to 50
- memory: bfloat16 [8, 128, 2, 5120], P('section', 'expert'), may hold values from -80 to 80
- cotangent: bfloat16 [8, 4096, 5120], P('section', 'expert'), may hold values from -6 to 6
- norm_gain: float32 [8, 5120], P('section'), may hold values from 0.5 to 1.5
- attn_gain: float32 [8, 5120], P('section'), may hold values from 0.5 to 1.5
- expert_in: bfloat16 [8, 5120, 10240], P('section', None, 'expert'), may hold values from -0.078125 to 0.078125
- expert_out: bfloat16 [8, 10240, 5120], P('section', 'expert'), may hold values from -0.0625 to 0.0625
- slot_index: int32 [8, 4096], P('section', 'expert'), may hold values from -1 to 7, as said below
- gate_prob: float32 [8, 4096], P('section', 'expert'), may hold values from 0.2 to 1
Outputs:
- layer_out: bfloat16 [8, 4096, 5120], P('section', 'expert')
- arriving: bfloat16 [8, 4096, 5120], P('section', 'expert')
- grad_memory: float32 [8, 128, 2, 5120], P('section', 'expert')
Inputs may be any that keep to these rules, and one draw needn't show every extreme that they name: `slot_index`: within each aligned block of 128 tokens of a layer the slots used are 0 to that block's count minus 1, each once; counts lie between 8 // 3 (at least 1) and 8, and every layer has a block with all 8 slots used.
All inputs are finite; a program needn't handle non-finite values.
Results may differ from a plain program's by a relative error of at most 0.0049.
The roundings to bfloat16 on the way count: a program that leaves them out, or rounds other values in their place, can miss the bound.
Values may be sent and summed in bfloat16 or wider, within the bound.
A program may use at most 128 MiB of HBM per device.

v0:
```python
import jax
import jax.numpy as jnp
from jax import lax
from jax.sharding import PartitionSpec as P

HD = 128
CAP = 8


def passed_along(block, axis, distance):
    devices = range(lax.axis_size(axis))
    route = [(i - distance, i) for i in devices if i - distance in devices]
    return lax.ppermute(block, axis, route)


def rms_scale(values, scale_row):
    return values * lax.rsqrt(jnp.mean(values * values, axis=-1, keepdims=True) + 1e-06) * scale_row


def attend_parts(per_head_queries, per_head_keys, per_head_values, incoming_head_gradient):
    scaling_factor = HD ** (-0.5)
    attention_scores = (
        jnp.einsum(
            "ksu,lsu->skl", per_head_queries, per_head_keys, preferred_element_type=jnp.float32
        )
        * scaling_factor
    )
    highest = jnp.max(attention_scores, axis=-1, keepdims=True)
    weights = jnp.exp(attention_scores - highest)
    weights = weights / jnp.sum(weights, axis=-1, keepdims=True)
    rounded_down = weights.astype(jnp.bfloat16)
    expert_mixture = jnp.einsum(
        "cif,fcv->icv", rounded_down, per_head_values, preferred_element_type=jnp.float32
    )
    probability_gradient = jnp.einsum(
        "ksu,lsu->skl", incoming_head_gradient, per_head_values, preferred_element_type=jnp.float32
    )
    dscore = (
        weights
        * (probability_gradient - jnp.sum(probability_gradient * weights, axis=-1, keepdims=True))
        * scaling_factor
    )
    upper_limit = dscore.astype(jnp.bfloat16)
    lower_limit = (dscore - upper_limit.astype(jnp.float32)).astype(jnp.bfloat16)
    return (
        expert_mixture.reshape(expert_mixture.shape[0], -1),
        rounded_down,
        upper_limit,
        lower_limit,
    )


def local(
    layer_in, memory, cotangent, norm_gain, attn_gain, expert_in, expert_out, slot_index, gate_prob
):
    sections = lax.axis_size("section")
    decoder = lax.axis_index("section") >= sections // 2
    sources = lax.all_gather(memory[0], "expert", axis=0, tiled=True)
    source_rows = sources.shape[0]
    per_head_keys = sources[:, 0].reshape(source_rows, -1, HD)
    per_head_values = sources[:, 1].reshape(source_rows, -1, HD)
    current = layer_in[0].astype(jnp.float32)
    queries = rms_scale(current, attn_gain[0]).astype(jnp.bfloat16)
    query_rows = queries.shape[0]
    per_head_queries = queries.reshape(query_rows, -1, HD)
    incoming_head_gradient = cotangent[0].reshape(query_rows, -1, HD)
    expert_mixture, rounded_down, upper_limit, lower_limit = attend_parts(
        per_head_queries, per_head_keys, per_head_values, incoming_head_gradient
    )
    decoder_mask = decoder.astype(jnp.float32)
    expert_mixture = expert_mixture * decoder_mask
    residual = (current + expert_mixture).astype(jnp.bfloat16)
    normed = rms_scale(residual.astype(jnp.float32), norm_gain[0]).astype(jnp.bfloat16)
    onehot = (slot_index[0][None, :] == jnp.arange(CAP, dtype=jnp.int32)[:, None]).astype(
        jnp.bfloat16
    )
    capacity = jnp.dot(onehot, normed, preferred_element_type=jnp.float32).astype(jnp.bfloat16)
    gathered = lax.all_gather(capacity, "expert", axis=0, tiled=True)
    hidden = jax.nn.gelu(
        jnp.dot(gathered, expert_in[0], preferred_element_type=jnp.float32)
    ).astype(jnp.bfloat16)
    returned = lax.psum_scatter(
        jnp.dot(hidden, expert_out[0], preferred_element_type=jnp.float32).astype(jnp.bfloat16),
        "expert",
        scatter_dimension=0,
        tiled=True,
    ).astype(jnp.float32)
    combined = jnp.dot(onehot.astype(jnp.float32).T, returned, precision=lax.Precision.HIGHEST)
    output = (residual.astype(jnp.float32) + gate_prob[0][:, None] * combined).astype(jnp.bfloat16)
    arriving = passed_along(output, "section", 1)
    value_gradient_rows = jnp.einsum(
        "yfg,fyb->gyb", rounded_down, incoming_head_gradient, preferred_element_type=jnp.float32
    )
    key_gradient_rows = jnp.einsum(
        "yfg,fyb->gyb", upper_limit, per_head_queries, preferred_element_type=jnp.float32
    )
    key_gradient_rows = key_gradient_rows + jnp.einsum(
        "yfg,fyb->gyb", lower_limit, per_head_queries, preferred_element_type=jnp.float32
    )
    stacked = jnp.stack(
        [key_gradient_rows.reshape(source_rows, -1), value_gradient_rows.reshape(source_rows, -1)],
        axis=1,
    )
    total_grad = lax.psum_scatter(stacked * decoder_mask, "expert", scatter_dimension=0, tiled=True)
    return (output[None], arriving[None], total_grad[None])


def solution(mesh):
    placed = (
        P("section", "expert", None),
        P("section", "expert", None, None),
        P("section", "expert", None),
        P("section", None),
        P("section", None),
        P("section", None, "expert"),
        P("section", "expert", None),
        P("section", "expert"),
        P("section", "expert"),
    )
    return jax.shard_map(
        local,
        mesh=mesh,
        in_specs=placed,
        out_specs=(
            P("section", "expert", None),
            P("section", "expert", None),
            P("section", "expert", None, None),
        ),
        check_vma=False,
    )
```

profile of v0, /device:TPU:64, one launch (start us, length us, event | category | flops | bytes accessed | tf_op | source)
XLA Modules:
  0.0 911.0 jit_solution(9836387654579746294)
XLA Ops:
  7.2 0.0 copy-start
  7.2 0.0 all-gather.6.cloned.1.call-start
  7.2 0.7 all-gather.6.cloned.1.call-update
  7.9 0.0 all-gather.4.cloned.1.call-start
  8.0 0.0 copy-start.6
  8.0 3.0 copy.61
  11.0 1.6 fusion.10
  12.7 0.0 copy-done.6
  12.7 3.1 multiply_convert_fusion
  15.8 157.1 %all-gather.6.cloned.1.call-done = bf16[1,128,2,5120]{3,2,0,1:T(2,128)(2,1)} async-done(((bf16[1,4,2,5120]{3,2,0,1:T(2,128)(2,1)}), bf16[1,128,2,5120]{3,2,0,1:T(2,128)(2,1)}) %all-gather.6.cloned.1.call-update) | async-done | bytes 2621456 | tf_op jit(solution)/shard_map/all_gather | solution.py:58
  172.9 7.4 copy.41
  180.3 3.4 fusion.68
  183.7 4.3 fusion.69
  188.0 4.2 convolution_multiply_fusion.1
  192.1 3.2 copy.45
  195.3 2.6 fusion.7
  198.0 0.0 copy-start.5
  198.0 1.0 copy-done.5
  199.0 0.0 copy-done.7
  199.0 0.0 copy-done.9
  199.0 1.1 convolution_convert_fusion.1
  200.2 0.0 all-gather.4.cloned.1.call-update
  200.2 0.0 reduce-scatter.2.cloned.1.call-start
  200.2 160.7 %all-gather.4.cloned.1.call-done = bf16[256,5120]{1,0:T(8,128)(2,1)} async-done(((bf16[8,5120]{1,0:T(8,128)(2,1)}), bf16[256,5120]{1,0:T(8,128)(2,1)}) %all-gather.4.cloned.1.call-update) | async-done | bytes 2621456 | tf_op jit(solution)/shard_map/all_gather | solution.py:78
  360.9 8.5 convolution_convert_fusion
  369.4 0.0 reduce-scatter.2.cloned.1.call-update
  369.5 0.2 all-reduce.3.cloned.1.call-start
  369.7 1.9 copy.62
  371.6 2.1 fusion.70
  373.7 7.1 fusion.23
  380.8 7.5 convolution_add_fusion
  388.3 5.0 copy.52
  393.3 4.6 fusion.33
  398.0 6.6 copy.53
  404.5 7.8 maximum_multiply_fusion
  412.3 0.0 all-reduce.3.cloned.1.call-update
  412.3 0.0 copy-start.10
  412.3 127.0 %reduce-scatter.2.cloned.1.call-done = bf16[8,5120]{1,0:T(8,128)(2,1)} async-done(((bf16[256,5120]{1,0:T(8,128)(2,1)}), bf16[8,5120]{1,0:T(8,128)(2,1)}) %reduce-scatter.2.cloned.1.call-update) | async-done | bytes 81936 | tf_op jit(solution)/shard_map/reduce_scatter | solution.py:82
  539.3 0.0 copy-done.8
  539.3 3.1 fusion.3
  542.4 1.9 collective-permute-start
  544.3 0.0 copy-done.10
  544.3 0.6 dynamic-slice
  545.6 354.8 %all-reduce.3.cloned.1.call-done = f32[128,2,5120]{2,1,0:T(2,128)} async-done(((f32[128,2,5120]{2,1,0:T(2,128)}), f32[128,2,5120]{2,1,0:T(2,128)}) %all-reduce.3.cloned.1.call-update) | async-done | bytes 5242896
  900.4 1.6 dynamic-slice_bitcast_fusion
  902.0 0.0 collective-permute-done
  902.0 2.5 copy.65
  904.5 0.0 copy-done.1
  (13 shorter events, 0.0 us)
Async XLA Ops:
  7.2 353.7 %copy-start = (bf16[1,320,5120]{2,1,0:T(8,128)(2,1)S(1)}, bf16[1,320,5120]{2,1,0:T(8,128)(2,1)}, u32[]{:S(2)}) copy-start(bf16[1,320,5120]{2,1,0:T(8,128)(2,1)} %param.15) | copy-start | bytes 9830404
  7.2 165.7 %all-gather.6.cloned.1.call-start = ((), (), s32[]{:S(2)}) async-start(), calls=%async_computation.3 | async-start | bytes 2703360 | tf_op jit(solution)/shard_map/all_gather | solution.py:58
  7.9 353.0 %all-gather.4.cloned.1.call-start = ((), (), s32[]{:S(2)}) async-start(), calls=%async_computation.1 | async-start | bytes 2703360 | tf_op jit(solution)/shard_map/all_gather | solution.py:78
  8.0 4.7 copy-start.6
  195.3 3.7 copy-start.7
  195.3 3.7 copy-start.9
  198.0 1.1 copy-start.5
  200.2 339.1 %reduce-scatter.2.cloned.1.call-start = ((), (), s32[]{:S(2)}) async-start(), calls=%async_computation.2 | async-start | bytes 2703360 | tf_op jit(solution)/shard_map/reduce_scatter | solution.py:82
  369.4 2.2 copy-start.2
  369.5 531.0 %all-reduce.3.cloned.1.call-start = ((), (), s32[]{:S(2)}) async-start(), calls=%async_computation.4 | async-start | bytes 10485760
  371.6 2.1 copy-start.3
  373.7 7.1 copy-start.4
  412.3 127.0 %copy-start.8 = (f32[1,128]{1,0:T(1,128)S(1)}, f32[1,128]{1,0:T(1,128)}, u32[]{:S(2)}) copy-start(f32[1,128]{1,0:T(1,128)} %param.17) | copy-start | bytes 1540
  412.3 132.0 %copy-start.10 = (u32[256]{0:T(256)S(1)}, u32[256]{0:T(256)}, u32[]{:S(2)}) copy-start(u32[256]{0:T(256)} %constant.39) | copy-start | bytes 3076
  539.3 365.2 %copy-start.1 = (bf16[1,320,5120]{2,1,0:T(8,128)(2,1)S(1)}, bf16[1,320,5120]{2,1,0:T(8,128)(2,1)}, u32[]{:S(2)}) copy-start(bf16[1,320,5120]{2,1,0:T(8,128)(2,1)} %param.15) | copy-start | bytes 9830404
  542.4 359.6 %collective-permute-start = (bf16[128,5120]{1,0:T(8,128)(2,1)}, bf16[128,5120]{1,0:T(8,128)(2,1)}, u32[]{:S(2)}, u32[]{:S(2)}) collective-permute-start(bf16[128,5120]{1,0:T(8,128)(2,1)} %fusion.3), channel_id=1, source_target_pairs={{0,32},{32,64},{64,96},{96,128},{128,160},{160,192},{192,224},{1,3... | collective-permute-start | bytes 3932168 | tf_op jit(solution)/shard_map/ppermute | solution.py:13
Sparse Core Ops, SparseCore 0:
  9.8 162.9 all-gather.5
  200.3 160.5 all-gather.3
  369.6 169.6 reduce-scatter.1
  541.8 358.5 all-reduce.2
where the time goes:
time: 912 us; the launch traced here: 911 us
  waiting for transfers between devices  800 us (88%)
  matrix products  42.6 us (5%)
  local copies, waits for them, and re-layouts  36.2 us (4%)
  other arithmetic  15.1 us (2%)
  between operations  14.5 us (2%)
    unnamed x5, waiting for transfers between devices  356 us
    all_gather x1, waiting for transfers between devices, local(): gathered = lax.all_gather(capacity, 'expert', axis=0, tiled=True)  161 us
    all_gather x1, waiting for transfers between devices, local(): sources = lax.all_gather(memory[0], 'expert', axis=0, tiled=True)  157 us
    reduce_scatter x1, waiting for transfers between devices, local(): lax.psum_scatter(jnp.dot(hidden, expert_out[0], preferred_element_type=jn...  127 us
  transfers between devices with their start and end apart: 5, of which 4 were waited for; matrix products, arithmetic and copies ran while one was open for 6% of the time, Pallas kernels for 0%

commit v1 on v0

v1 whole, which is shorter than its diff:
```python
import jax
import jax.numpy as jnp
from jax import lax
from jax.experimental import pallas as pl
from jax.experimental.pallas import tpu as pltpu
from jax.sharding import PartitionSpec as P

HD = 128
CAP = 8
RING = 4
MESH = pl.DeviceIdType.MESH
BF = jnp.bfloat16
F32 = jnp.float32
NT = (((1,), (1,)), ((), ()))
TN = (((0,), (0,)), ((), ()))


def dot(a, b, dims=(((1,), (0,)), ((), ()))):
    return lax.dot_general(a, b, dims, preferred_element_type=F32)


class Links:
    def __init__(self, send, recv, section, x, y, z):
        self.send, self.recv = send, recv
        self.section, self.x, self.y, self.z = section, x, y, z
        self.started = []

    def copy(self, key, src, dst, device):
        return pltpu.make_async_remote_copy(
            src_ref=src,
            dst_ref=dst,
            send_sem=self.send.at[key],
            recv_sem=self.recv.at[key],
            device_id=device,
            device_id_type=MESH,
        )

    def put(self, key, src, dst, device):
        copy = self.copy(key, src, dst, device)
        copy.start()
        self.started.append(copy)

    def got(self, key, dst, device):
        self.copy(key, dst, dst, device).wait_recv()

    def finish(self):
        for copy in self.started:
            copy.wait_send()
        self.started = []


class Half:
    def __init__(self, links, first, lane, width):
        self.links, self.first, self.lane, self.width = links, first, lane, width
        self.u, self.v = (links.x, links.y) if first == "x" else (links.y, links.x)

    def at(self, buf, u, v, low=0, size=None):
        lanes = pl.ds(self.lane + low, self.width if size is None else size)
        if self.first == "x":
            return buf.at[u, v, :, :, lanes]
        return buf.at[v, u, :, :, lanes]

    def device(self, u, v):
        x, y = (u, v) if self.first == "x" else (v, u)
        return (self.links.section, x * (RING * 2) + y * 2 + self.links.z)


def step(i, by):
    return lax.rem(i + by + RING, RING)


GATHER_KEYS = 41
SCATTER_KEYS = 41


def gather(links, halves, buf, base):
    x, y, z = links.x, links.y, links.z
    pair = (links.section, x * (RING * 2) + y * 2 + (1 - z))
    links.put(base, buf.at[x, y, z], buf.at[x, y, z], pair)
    yield
    links.got(base, buf.at[x, y, 1 - z], pair)

    def spread(half, key, slot, u):
        part = half.at(buf, u, half.v)
        for turn in (1, -1):
            links.put(
                key + 4 + slot * 4 + (turn < 0),
                part,
                part,
                half.device(half.u, step(half.v, turn)),
            )

    def relay(half, key, slot, u):
        q = half.width // 2
        for turn in (1, -1):
            left = step(half.v, -turn)
            k = key + 4 + slot * 4 + (turn < 0)
            links.got(k, half.at(buf, u, left), half.device(half.u, left))
            part = half.at(buf, u, left, 0 if turn > 0 else q, q)
            links.put(k + 2, part, part, half.device(half.u, step(half.v, turn)))

    keyed = [(half, base + 1 + 20 * i) for i, half in enumerate(halves)]
    for half, key in keyed:
        part = half.at(buf, half.u, half.v)
        for turn in (1, -1):
            links.put(key + (turn < 0), part, part, half.device(step(half.u, turn), half.v))
    for half, key in keyed:
        spread(half, key, 0, half.u)
    yield
    for half, key in keyed:
        q = half.width // 2
        for slot, turn in ((1, 1), (2, -1)):
            left = step(half.u, -turn)
            links.got(key + (turn < 0), half.at(buf, left, half.v), half.device(left, half.v))
            part = half.at(buf, left, half.v, 0 if turn > 0 else q, q)
            links.put(key + 2 + (turn < 0), part, part, half.device(step(half.u, turn), half.v))
            spread(half, key, slot, left)
    yield
    for half, key in keyed:
        relay(half, key, 0, half.u)
    yield
    for half, key in keyed:
        q = half.width // 2
        far = step(half.u, 2)
        for turn in (1, -1):
            part = half.at(buf, far, half.v, 0 if turn > 0 else q, q)
            links.got(key + 2 + (turn < 0), part, half.device(step(half.u, -turn), half.v))
        spread(half, key, 3, far)
    yield
    for half, key in keyed:
        relay(half, key, 1, step(half.u, -1))
        relay(half, key, 2, step(half.u, 1))
    yield
    for half, key in keyed:
        relay(half, key, 3, step(half.u, 2))
    yield
    for half, key in keyed:
        q = half.width // 2
        for slot, by in ((0, 0), (1, -1), (2, 1), (3, 2)):
            for turn in (1, -1):
                part = half.at(
                    buf, step(half.u, by), step(half.v, 2), 0 if turn > 0 else q, q
                )
                links.got(
                    key + 4 + slot * 4 + 2 + (turn < 0),
                    part,
                    half.device(half.u, step(half.v, -turn)),
                )


def add_into(target, *others):
    total = target[...].astype(F32)
    for other in others:
        total = total + other[...].astype(F32)
    target[...] = total.astype(target.dtype)


def scatter(links, halves, buf, land, base):
    passing2, whole2, passing1, whole1, last = land
    x, y, z = links.x, links.y, links.z
    order = ((0, 2), (1, -1), (2, 1), (3, 0))
    keyed = [(i, half, base + 1 + 20 * i) for i, half in enumerate(halves)]
    for slot, by in order:
        for i, half, key in keyed:
            q = half.width // 2
            for turn in (1, -1):
                d = int(turn < 0)
                links.put(
                    key + slot * 4 + d,
                    half.at(buf, step(half.u, by), step(half.v, 2), d * q, q),
                    passing2.at[i, slot, d],
                    half.device(half.u, step(half.v, turn)),
                )
    yield
    for slot, by in order:
        for i, half, key in keyed:
            q = half.width // 2
            for turn in (1, -1):
                d = int(turn < 0)
                to = step(half.v, turn)
                links.got(
                    key + slot * 4 + d,
                    passing2.at[i, slot, d],
                    half.device(half.u, step(half.v, -turn)),
                )
                add_into(
                    half.at(buf, step(half.u, by), to, d * q, q), passing2.at[i, slot, d]
                )
                links.put(
                    key + slot * 4 + 2 + d,
                    half.at(buf, step(half.u, by), to),
                    whole2.at[i, slot, d],
                    half.device(half.u, to),
                )
        yield
    for slot, by in order:
        for i, half, key in keyed:
            q = half.width // 2
            for d, turn in ((0, 1), (1, -1)):
                links.got(
                    key + slot * 4 + 2 + d,
                    whole2.at[i, slot, d],
                    half.device(half.u, step(half.v, -turn)),
                )
            add_into(
                half.at(buf, step(half.u, by), half.v),
                whole2.at[i, slot, 0],
                whole2.at[i, slot, 1],
            )
            if by == 2:
                for d, turn in ((0, 1), (1, -1)):
                    links.put(
                        key + 16 + d,
                        half.at(buf, step(half.u, 2), half.v, d * q, q),
                        passing1.at[i, d],
                        half.device(step(half.u, turn), half.v),
                    )
            if by == 1:
                for d, turn in ((0, 1), (1, -1)):
                    to = step(half.u, turn)
                    links.got(
                        key + 16 + d, passing1.at[i, d], half.device(step(half.u, -turn), half.v)
                    )
                    add_into(half.at(buf, to, half.v, d * q, q), passing1.at[i, d])
                    links.put(
                        key + 18 + d,
                        half.at(buf, to, half.v),
                        whole1.at[i, d],
                        half.device(to, half.v),
                    )
        yield
    for i, half, key in keyed:
        for d, turn in ((0, 1), (1, -1)):
            links.got(key + 18 + d, whole1.at[i, d], half.device(step(half.u, -turn), half.v))
        add_into(half.at(buf, half.u, half.v), whole1.at[i, 0], whole1.at[i, 1])
    pair = (links.section, x * (RING * 2) + y * 2 + (1 - z))
    links.put(base, buf.at[x, y, 1 - z], last, pair)
    yield
    links.got(base, last, pair)


def drive(streams, tasks=()):
    streams, tasks = list(streams), list(tasks)
    while streams or tasks:
        for stream in list(streams):
            if next(stream, "end") == "end":
                streams.remove(stream)
        if tasks:
            tasks.pop(0)()


def scaled(rows, gain):
    return rows * lax.rsqrt(jnp.mean(rows * rows, axis=-1, keepdims=True) + 1e-06) * gain


def kernel(
    sections,
    mem_ref,
    layer_ref,
    cot_ref,
    norm_ref,
    attn_ref,
    in_ref,
    out_ref,
    slot_ref,
    gate_ref,
    layer_out,
    arriving,
    grad_out,
    cur,
    cot,
    win,
    wout,
    queries,
    resid,
    before,
    gkv,
    keys,
    values,
    gcap,
    probs,
    parts,
    gparts,
    dkeys,
    dvalues,
    picked,
    pickedq,
    attended,
    perm,
    perm_t,
    hacc,
    hidden,
    own_slot,
    their_slot,
    own_rows,
    their_rows,
    land_a,
    land_b,
    land_c,
    land_d,
    land_e,
    glast,
    gland_a,
    gland_b,
    gland_c,
    gland_d,
    load_sem,
    send_sem,
    recv_sem,
):
    tokens, width = cur.shape
    half_width = width // 2
    heads = width // HD
    ffw = win.shape[1]
    scaling_factor = HD ** (-0.5)
    section = lax.axis_index("section")
    place = lax.axis_index("expert")
    x, y, z = place // (RING * 2), (place // 2) % RING, place % 2
    links = Links(send_sem, recv_sem, section, x, y, z)
    halves = (
        Half(links, "x", 0, half_width // 2),
        Half(links, "y", half_width // 2, half_width // 2),
    )
    cap_base, kv_base = 0, GATHER_KEYS
    ret_base = kv_base + GATHER_KEYS
    grad_base = ret_base + SCATTER_KEYS
    pass_base = grad_base + SCATTER_KEYS

    loads = [
        pltpu.make_async_copy(src, dst, load_sem.at[i])
        for i, (src, dst) in enumerate(
            ((layer_ref, cur), (cot_ref, cot), (in_ref, win), (out_ref, wout))
        )
    ]
    for load in loads:
        load.start()

    def device(xx, yy, zz):
        return (section, xx * (RING * 2) + yy * 2 + zz)

    barrier = pltpu.get_barrier_semaphore()
    for peer in (
        device(x, y, 1 - z),
        device(step(x, 1), y, z),
        device(step(x, -1), y, z),
        device(x, step(y, 1), z),
        device(x, step(y, -1), z),
    ):
        pl.semaphore_signal(barrier, inc=1, device_id=peer, device_id_type=MESH)

    @pl.when(section > 0)
    def _():
        pl.semaphore_signal(
            barrier, inc=1, device_id=(section - 1, place), device_id_type=MESH
        )

    @pl.when(section < sections - 1)
    def _():
        pl.semaphore_signal(
            barrier, inc=1, device_id=(section + 1, place), device_id_type=MESH
        )

    ends = jnp.where(section > 0, 1, 0) + jnp.where(section < sections - 1, 1, 0)
    pl.semaphore_wait(barrier, 5 + ends)

    def pass_copy(key, src, dst):
        return links.copy(pass_base + key, src, dst, (section + 1, place))

    def pass_on(key, src, dst):
        @pl.when(section < sections - 1)
        def _():
            pass_copy(key, src, dst).start()

    def pass_sent(key, src, dst):
        @pl.when(section < sections - 1)
        def _():
            pass_copy(key, src, dst).wait_send()

    def pass_got(key, dst):
        @pl.when(section > 0)
        def _():
            links.copy(pass_base + key, dst, dst, (section - 1, place)).wait_recv()

    slots = slot_ref[...]
    rows16 = lax.broadcasted_iota(jnp.int32, (2 * CAP, tokens), 0)
    onehot = (slots == rows16).astype(F32).astype(BF)
    has_row = jnp.sum((slots == rows16).astype(F32), axis=-1, keepdims=True)

    def pick(source, target):
        def one(i, carry):
            lanes = pl.ds(pl.multiple_of(i * 512, 512), 512)
            target[:, lanes] = dot(onehot, source[:, lanes]).astype(target.dtype)
            return carry

        lax.fori_loop(0, width // 512, one, 0)

    def fold(rows):
        return jnp.concatenate([rows[:CAP, :half_width], rows[:CAP, half_width:]], axis=0)

    def put_capacity():
        rows = picked[...].astype(F32)
        gcap[x, y, z] = fold(scaled(rows, norm_ref[...])).astype(BF)

    def expert():
        loads[2].wait()
        loads[3].wait()
        hacc[...] = jnp.zeros_like(hacc)

        def into(k, carry):
            lanes = pl.ds(pl.multiple_of(k * 256, 256), 256)
            block = gcap[:, :, :, :, lanes].reshape(-1, 256)
            low = dot(block, win[lanes, :])
            high_rows = pl.ds(pl.multiple_of(half_width + k * 256, 256), 256)
            high = dot(block, win[high_rows, :])
            low = low.reshape(-1, 2 * CAP, ffw)[:, :CAP]
            high = high.reshape(-1, 2 * CAP, ffw)[:, CAP:]
            hacc[...] += low + high
            return carry

        lax.fori_loop(0, half_width // 256, into, 0)
        hidden[...] = jax.nn.gelu(hacc[...].reshape(-1, ffw)).astype(BF)

        def out(k, carry):
            lanes = pl.ds(pl.multiple_of(k * 256, 256), 256)
            high_lanes = pl.ds(pl.multiple_of(half_width + k * 256, 256), 256)
            low = dot(hidden[...], wout[:, lanes]).reshape(-1, CAP, 256)
            high = dot(hidden[...], wout[:, high_lanes]).reshape(-1, CAP, 256)
            block = jnp.concatenate([low, high], axis=1).astype(BF)
            parts[:, :, :, :, lanes] = block.reshape(RING, RING, 2, 2 * CAP, 256)
            return carry

        lax.fori_loop(0, half_width // 256, out, 0)

    ret_land = (land_a, land_b, land_c, land_d, land_e)

    def spread_rows(slot_rows, rows, base, target):
        lane_rows = lax.broadcasted_iota(jnp.int32, (2 * CAP, tokens), 0)
        low = (slot_rows == lane_rows).astype(F32).astype(BF)
        high = (slot_rows == lane_rows - CAP).astype(F32)
        high = jnp.where(lane_rows < CAP, 0.0, high).astype(BF)
        has = dot(low, jnp.ones((2 * CAP, 128), BF), TN)[:, :1] > 0.5
        for chosen, start in ((low, 0), (high, half_width)):

            def one(i, carry, chosen=chosen, start=start):
                lanes = pl.ds(pl.multiple_of(i * 512, 512), 512)
                full = pl.ds(pl.multiple_of(start + i * 512, 512), 512)
                moved = dot(chosen, rows[:, lanes], TN)
                kept = base[:, full].astype(F32)
                target[:, full] = jnp.where(has, moved, kept).astype(BF)
                return carry

            lax.fori_loop(0, half_width // 512, one, 0)

    def finish(base):
        returned = parts[x, y, z].astype(F32) + land_e[...].astype(F32)
        gates = jnp.sum(
            jnp.where(slots == rows16[:CAP], gate_ref[...], 0.0), axis=-1, keepdims=True
        )
        gates = jnp.concatenate([gates, gates], axis=0)
        own_rows[...] = (fold(picked[...].astype(F32)) + gates * returned).astype(BF)
        pass_on(2, own_rows, their_rows)
        spread_rows(slots, own_rows, base, layer_out)
        pass_got(0, before)
        pass_got(1, their_slot)
        pass_got(2, their_rows)

        @pl.when(section > 0)
        def _():
            spread_rows(their_slot[:1, :], their_rows, before, arriving)

        @pl.when(section == 0)
        def _():
            arriving[...] = jnp.zeros_like(arriving)

        pass_sent(0, base, before)
        pass_sent(1, own_slot, their_slot)
        pass_sent(2, own_rows, their_rows)

    own_slot[...] = jnp.broadcast_to(slots, own_slot.shape)

    @pl.when(section < sections // 2)
    def _():
        loads[0].wait()
        pick(cur, picked)
        put_capacity()
        stream = gather(links, halves, gcap, cap_base)
        next(stream)
        pass_on(0, cur, before)
        pass_on(1, own_slot, their_slot)
        drive([stream])
        loads[1].wait()
        expert()
        drive([scatter(links, halves, parts, ret_land, ret_base)])
        grad_out[...] = jnp.zeros_like(grad_out)
        finish(cur)
        links.finish()

    @pl.when(section >= sections // 2)
    def _():
        gkv[x, y, z] = mem_ref[...]

        def make_perm():
            for target, flip in ((perm, 0), (perm_t, 1)):
                k = lax.broadcasted_iota(jnp.int32, (256, 256), flip)
                i = lax.broadcasted_iota(jnp.int32, (256, 256), 1 - flip)
                m = k & 63
                source = ((m >> 2) << 4) + ((k >> 7) << 3) + ((m & 3) << 1) + ((k >> 6) & 1)
                target[...] = (source == i).astype(F32).astype(BF)

        def make_queries():
            loads[0].wait()

            def one(i, carry):
                rows = pl.ds(pl.multiple_of(i * 16, 16), 16)
                queries[rows, :] = scaled(cur[rows, :].astype(F32), attn_ref[...]).astype(BF)
                return carry

            lax.fori_loop(0, tokens // 16, one, 0)

        def pick_rows():
            pick(cur, picked)
            pick(queries, pickedq)

        drive(
            [gather(links, halves, gkv, kv_base)],
            [lambda: pass_on(1, own_slot, their_slot), make_perm, make_queries, pick_rows],
        )

        for c in range(2):

            def sort_in(i, carry, c=c):
                lanes = pl.ds(pl.multiple_of(i * 256, 256), 256)
                high = pl.ds(pl.multiple_of(half_width + i * 256, 256), 256)
                block = gkv[2 * c : 2 * c + 2, :, :, :, lanes].reshape(256, 256)
                block = dot(perm[...], block).astype(BF)
                keys[64 * c : 64 * c + 64, lanes] = block[:64]
                values[64 * c : 64 * c + 64, lanes] = block[64:128]
                keys[64 * c : 64 * c + 64, high] = block[128:192]
                values[64 * c : 64 * c + 64, high] = block[192:]
                return carry

            lax.fori_loop(0, half_width // 256, sort_in, 0)

        def chosen_heads(group, carry):
            for j in range(4):
                lanes = pl.ds(pl.multiple_of((group * 4 + j) * HD, HD), HD)
                scores = dot(pickedq[:, lanes], keys[:, lanes], NT) * scaling_factor
                weights = jnp.exp(scores - jnp.max(scores, axis=-1, keepdims=True))
                weights = weights / jnp.sum(weights, axis=-1, keepdims=True)
                mixed = dot(weights.astype(BF), values[:, lanes])
                attended[:, lanes] = picked[:, lanes].astype(F32) + mixed * has_row
            return carry

        lax.fori_loop(0, heads // 4, chosen_heads, 0)
        picked[...] = attended[...].astype(BF)
        put_capacity()

        def forward(group, carry):
            for j in range(4):
                head = group * 4 + j
                lanes = pl.ds(pl.multiple_of(head * HD, HD), HD)
                scores = dot(keys[:, lanes], queries[:, lanes], NT) * scaling_factor
                weights = jnp.exp(scores - jnp.max(scores, axis=0, keepdims=True))
                weights = weights / jnp.sum(weights, axis=0, keepdims=True)
                probs[head] = weights
                mixed = dot(weights.astype(BF), values[:, lanes], TN)
                resid[:, lanes] = (cur[:, lanes].astype(F32) + mixed).astype(BF)
            return carry

        def backward(group, carry):
            for j in range(4):
                head = group * 4 + j
                lanes = pl.ds(pl.multiple_of(head * HD, HD), HD)
                weights = probs[head]
                upstream = cot[:, lanes]
                asked = queries[:, lanes]
                dweights = dot(values[:, lanes], upstream, NT)
                inner = jnp.sum(dweights * weights, axis=0, keepdims=True)
                dscores = weights * (dweights - inner) * scaling_factor
                high = dscores.astype(BF)
                low = (dscores - high.astype(F32)).astype(BF)
                dkeys[:, lanes] = dot(
                    jnp.concatenate([high, low], axis=1),
                    jnp.concatenate([asked, asked], axis=0),
                ).astype(BF)
                dvalues[:, lanes] = dot(weights.astype(BF), upstream).astype(BF)
            return carry

        def part_of(work, i, of):
            count = heads // 4

            def task():
                lax.fori_loop(count * i // of, count * (i + 1) // of, work, 0)

            return task

        def hand_over():
            pass_on(0, resid, before)
            loads[1].wait()

        drive(
            [gather(links, halves, gcap, cap_base)],
            [part_of(forward, i, 4) for i in range(4)]
            + [hand_over]
            + [part_of(backward, i, 4) for i in range(4)],
        )

        for c in range(2):

            def sort_out(i, carry, c=c):
                lanes = pl.ds(pl.multiple_of(i * 256, 256), 256)
                high = pl.ds(pl.multiple_of(half_width + i * 256, 256), 256)
                rows = slice(64 * c, 64 * c + 64)
                block = jnp.concatenate(
                    [dkeys[rows, lanes], dvalues[rows, lanes], dkeys[rows, high], dvalues[rows, high]],
                    axis=0,
                )
                block = dot(perm_t[...], block).astype(BF)
                gparts[2 * c : 2 * c + 2, :, :, :, lanes] = block.reshape(
                    2, RING, 2, 2 * CAP, 256
                )
                return carry

            lax.fori_loop(0, half_width // 256, sort_out, 0)

        grad_stream = scatter(
            links, halves, gparts, (gland_a, gland_b, gland_c, gland_d, glast), grad_base
        )
        next(grad_stream)
        expert()
        drive([scatter(links, halves, parts, ret_land, ret_base), grad_stream])
        total = gparts[x, y, z].astype(F32) + glast[...].astype(F32)
        grad_out[...] = jnp.concatenate([total[:CAP], total[CAP:]], axis=1)
        finish(resid)
        links.finish()


def local(
    layer_in, memory, cotangent, norm_gain, attn_gain, expert_in, expert_out, slot_index, gate_prob
):
    sections = lax.axis_size("section")
    tokens, width = layer_in.shape[1:]
    rows = memory.shape[1]
    stash = rows * 2 * RING * RING
    ffw = expert_in.shape[2]
    half = width // 2
    heads = width // HD
    mem = memory[0].reshape(rows * 2, 2, half).transpose(1, 0, 2).reshape(rows * 4, half)
    vmem = pl.BlockSpec(memory_space=pltpu.VMEM)
    anywhere = pl.BlockSpec(memory_space=pl.ANY)
    full = (RING, RING, 2, 2 * CAP, half)
    quarter = half // 4
    landing = [
        pltpu.VMEM((2, RING, 2, 2, 2 * CAP, quarter), BF),
        pltpu.VMEM((2, RING, 2, 2, 2 * CAP, 2 * quarter), BF),
        pltpu.VMEM((2, 2, 2, 2 * CAP, quarter), BF),
        pltpu.VMEM((2, 2, 2, 2 * CAP, 2 * quarter), BF),
    ]
    count = 2 * GATHER_KEYS + 2 * SCATTER_KEYS + 3
    layer_out, arriving, grad = pl.pallas_call(
        lambda *refs: kernel(sections, *refs),
        out_shape=(
            jax.ShapeDtypeStruct((tokens, width), BF),
            jax.ShapeDtypeStruct((tokens, width), BF),
            jax.ShapeDtypeStruct((rows * 2, width), F32),
        ),
        in_specs=[vmem, anywhere, anywhere, vmem, vmem, anywhere, anywhere, vmem, vmem],
        out_specs=(vmem, vmem, vmem),
        scratch_shapes=[
            pltpu.VMEM((tokens, width), BF),
            pltpu.VMEM((tokens, width), BF),
            pltpu.VMEM((width, ffw), BF),
            pltpu.VMEM((ffw, width), BF),
            pltpu.VMEM((tokens, width), BF),
            pltpu.VMEM((tokens, width), BF),
            pltpu.VMEM((tokens, width), BF),
            pltpu.VMEM(full, BF),
            pltpu.VMEM((stash, width), BF),
            pltpu.VMEM((stash, width), BF),
            pltpu.VMEM(full, BF),
            pltpu.VMEM((heads, stash, tokens), F32),
            pltpu.VMEM(full, BF),
            pltpu.VMEM(full, BF),
            pltpu.VMEM((stash, width), BF),
            pltpu.VMEM((stash, width), BF),
            pltpu.VMEM((2 * CAP, width), BF),
            pltpu.VMEM((2 * CAP, width), BF),
            pltpu.VMEM((2 * CAP, width), F32),
            pltpu.VMEM((256, 256), BF),
            pltpu.VMEM((256, 256), BF),
            pltpu.VMEM((2 * RING * RING, CAP, ffw), F32),
            pltpu.VMEM((2 * RING * RING * CAP, ffw), BF),
            pltpu.VMEM((8, tokens), jnp.int32),
            pltpu.VMEM((8, tokens), jnp.int32),
            pltpu.VMEM((2 * CAP, half), BF),
            pltpu.VMEM((2 * CAP, half), BF),
            *landing,
            pltpu.VMEM((2 * CAP, half), BF),
            pltpu.VMEM((2 * CAP, half), BF),
            *landing,
            pltpu.SemaphoreType.DMA((4,)),
            pltpu.SemaphoreType.DMA((count,)),
            pltpu.SemaphoreType.DMA((count,)),
        ],
        compiler_params=pltpu.CompilerParams(
            collective_id=0, has_side_effects=True, vmem_limit_bytes=60 * 1024 * 1024
        ),
    )(
        mem,
        layer_in[0],
        cotangent[0],
        norm_gain,
        attn_gain,
        expert_in[0],
        expert_out[0],
        slot_index,
        gate_prob,
    )
    return (layer_out[None], arriving[None], grad.reshape(1, rows, 2, width))


def solution(mesh):
    placed = (
        P("section", "expert", None),
        P("section", "expert", None, None),
        P("section", "expert", None),
        P("section", None),
        P("section", None),
        P("section", None, "expert"),
        P("section", "expert", None),
        P("section", "expert"),
        P("section", "expert"),
    )
    return jax.shard_map(
        local,
        mesh=mesh,
        in_specs=placed,
        out_specs=(
            P("section", "expert", None),
            P("section", "expert", None),
            P("section", "expert", None, None),
        ),
        check_vma=False,
    )
```

time: 912 us -> 133 us (0.15)
  the two profiles are of different devices: /device:TPU:64 before, /device:TPU:129 now
where the time goes in v1:
time: 133 us; the launch traced here: 132 us
  Pallas kernels  119 us (89%)
  local copies, waits for them, and re-layouts  12.7 us (10%)
    pallas_call x1, Pallas kernels, local(): pl.pallas_call(lambda *refs: kernel(sections, *refs), out_shape=(jax.Shap...  119 us
    unnamed x5, local copies, waits for them, and re-layouts  9.45 us

profile of v1, /device:TPU:129, one launch (start us, length us, event | category | flops | bytes accessed | tf_op | source)
XLA Modules:
  0.0 132.2 jit_solution(2252981169203920604)
XLA Ops:
  0.6 0.9 reshape_squeeze.3
  1.6 0.6 copy.15
  2.2 5.8 %copy.13 = bf16[1,5120,320]{2,1,0:T(8,128)(2,1)} copy(bf16[1,5120,320]{1,2,0:T(8,128)(2,1)} %param.14) | data formatting | bytes 6553600 | tf_op args[5]
  8.1 118.8 %shard_map.112 = (bf16[128,5120]{1,0:T(8,128)(2,1)}, bf16[128,5120]{1,0:T(8,128)(2,1)}, f32[8,5120]{1,0:T(8,128)}) custom-call(bf16[16,2560]{1,0:T(8,128)(2,1)} %bitcast.17, bf16[128,5120]{1,0:T(8,128)(2,1)} %bitcast.13, bf16[128,5120]{1,0:T(8,128)(2,1)} %bitcast.14, f32[1,5120]{1,0:T(1,128)} %refs_3_.1, f32[1,5120]{1,0:T(1,128)} %refs_4_.1, ...), custom_call_target="tpu_custom_call" | custom-call | tf_op jit(solution)/shard_map/pallas_call | solution.py:660
  126.9 1.7 %reshape.13 = f32[1,4,2,5120]{3,2,1,0:T(2,128)} reshape(f32[8,5120]{1,0:T(8,128)} %get-tuple-element.8) | data formatting | bytes 327680 | tf_op jit(solution)/shard_map/reshape | solution.py:719
  128.6 0.0 copy-start
  128.6 2.6 %copy.18 = bf16[1,128,5120]{2,1,0:T(8,128)(2,1)} copy(bf16[1,128,5120]{2,1,0:T(8,128)(2,1)} %bitcast.16) | data formatting | bytes 2621440
  131.1 0.0 copy-done
  131.1 1.1 copy.19
Async XLA Ops:
  128.6 2.6 %copy-start = (bf16[128,5120]{1,0:T(8,128)(2,1)S(1)}, bf16[128,5120]{1,0:T(8,128)(2,1)}, u32[]{:S(2)}) copy-start(bf16[128,5120]{1,0:T(8,128)(2,1)} %get-tuple-element.7) | copy-start | bytes 3932164

commit v2 on v1

--- a/solution.py
+++ b/solution.py
@@ -264,8 +264,11 @@
     out_ref,
     slot_ref,
     gate_ref,
-    layer_out,
-    arriving,
+    base_out,
+    before,
+    own_rows,
+    their_rows,
+    their_slot,
     grad_out,
     cur,
     cot,
@@ -273,7 +276,6 @@
     wout,
     queries,
     resid,
-    before,
     gkv,
     keys,
     values,
@@ -291,9 +293,6 @@
     hacc,
     hidden,
     own_slot,
-    their_slot,
-    own_rows,
-    their_rows,
     land_a,
     land_b,
     land_c,
@@ -311,7 +310,7 @@
     tokens, width = cur.shape
     half_width = width // 2
     heads = width // HD
-    ffw = win.shape[1]
+    ffw = win.shape[0]
     scaling_factor = HD ** (-0.5)
     section = lax.axis_index("section")
     place = lax.axis_index("expert")
@@ -409,9 +408,9 @@
         def into(k, carry):
             lanes = pl.ds(pl.multiple_of(k * 256, 256), 256)
             block = gcap[:, :, :, :, lanes].reshape(-1, 256)
-            low = dot(block, win[lanes, :])
-            high_rows = pl.ds(pl.multiple_of(half_width + k * 256, 256), 256)
-            high = dot(block, win[high_rows, :])
+            high_lanes = pl.ds(pl.multiple_of(half_width + k * 256, 256), 256)
+            low = dot(block, win[:, lanes], NT)
+            high = dot(block, win[:, high_lanes], NT)
             low = low.reshape(-1, 2 * CAP, ffw)[:, :CAP]
             high = high.reshape(-1, 2 * CAP, ffw)[:, CAP:]
             hacc[...] += low + high
@@ -433,24 +432,6 @@
 
     ret_land = (land_a, land_b, land_c, land_d, land_e)
 
-    def spread_rows(slot_rows, rows, base, target):
-        lane_rows = lax.broadcasted_iota(jnp.int32, (2 * CAP, tokens), 0)
-        low = (slot_rows == lane_rows).astype(F32).astype(BF)
-        high = (slot_rows == lane_rows - CAP).astype(F32)
-        high = jnp.where(lane_rows < CAP, 0.0, high).astype(BF)
-        has = dot(low, jnp.ones((2 * CAP, 128), BF), TN)[:, :1] > 0.5
-        for chosen, start in ((low, 0), (high, half_width)):
-
-            def one(i, carry, chosen=chosen, start=start):
-                lanes = pl.ds(pl.multiple_of(i * 512, 512), 512)
-                full = pl.ds(pl.multiple_of(start + i * 512, 512), 512)
-                moved = dot(chosen, rows[:, lanes], TN)
-                kept = base[:, full].astype(F32)
-                target[:, full] = jnp.where(has, moved, kept).astype(BF)
-                return carry
-
-            lax.fori_loop(0, half_width // 512, one, 0)
-
     def finish(base):
         returned = parts[x, y, z].astype(F32) + land_e[...].astype(F32)
         gates = jnp.sum(
@@ -459,24 +440,19 @@
         gates = jnp.concatenate([gates, gates], axis=0)
         own_rows[...] = (fold(picked[...].astype(F32)) + gates * returned).astype(BF)
         pass_on(2, own_rows, their_rows)
-        spread_rows(slots, own_rows, base, layer_out)
         pass_got(0, before)
         pass_got(1, their_slot)
         pass_got(2, their_rows)
 
-        @pl.when(section > 0)
-        def _():
-            spread_rows(their_slot[:1, :], their_rows, before, arriving)
-
-        @pl.when(section == 0)
-        def _():
-            arriving[...] = jnp.zeros_like(arriving)
-
         pass_sent(0, base, before)
         pass_sent(1, own_slot, their_slot)
         pass_sent(2, own_rows, their_rows)
 
     own_slot[...] = jnp.broadcast_to(slots, own_slot.shape)
+    nothing = pltpu.make_async_copy(resid, before, load_sem.at[5])
+
+    def keep(base):
+        return pltpu.make_async_copy(base, base_out, load_sem.at[4])
 
     @pl.when(section < sections // 2)
     def _():
@@ -487,17 +463,33 @@
         next(stream)
         pass_on(0, cur, before)
         pass_on(1, own_slot, their_slot)
+        keep(cur).start()
+
+        @pl.when(section == 0)
+        def _():
+            resid[...] = jnp.zeros_like(resid)
+            nothing.start()
+            their_slot[...] = jnp.full_like(their_slot, -1)
+            their_rows[...] = jnp.zeros_like(their_rows)
+
         drive([stream])
         loads[1].wait()
         expert()
         drive([scatter(links, halves, parts, ret_land, ret_base)])
         grad_out[...] = jnp.zeros_like(grad_out)
         finish(cur)
+        keep(cur).wait()
+
+        @pl.when(section == 0)
+        def _():
+            nothing.wait()
+
         links.finish()
 
     @pl.when(section >= sections // 2)
     def _():
-        gkv[x, y, z] = mem_ref[...]
+        rows = [mem_ref[r].astype(F32) for r in range(mem_ref.shape[0])]
+        gkv[x, y, z] = fold(jnp.concatenate(rows, axis=0)).astype(BF)
 
         def make_perm():
             for target, flip in ((perm, 0), (perm_t, 1)):
@@ -541,49 +533,64 @@
 
             lax.fori_loop(0, half_width // 256, sort_in, 0)
 
+        def heads_of(block, count):
+            return [block[:, j * HD : (j + 1) * HD] for j in range(count)]
+
         def chosen_heads(group, carry):
-            for j in range(4):
-                lanes = pl.ds(pl.multiple_of((group * 4 + j) * HD, HD), HD)
-                scores = dot(pickedq[:, lanes], keys[:, lanes], NT) * scaling_factor
-                weights = jnp.exp(scores - jnp.max(scores, axis=-1, keepdims=True))
-                weights = weights / jnp.sum(weights, axis=-1, keepdims=True)
-                mixed = dot(weights.astype(BF), values[:, lanes])
-                attended[:, lanes] = picked[:, lanes].astype(F32) + mixed * has_row
+            lanes = pl.ds(pl.multiple_of(group * (8 * HD), 8 * HD), 8 * HD)
+            asked, kept = heads_of(pickedq[:, lanes], 8), heads_of(keys[:, lanes], 8)
+            scores = [dot(q, k, NT) for q, k in zip(asked, kept)]
+            scores = jnp.concatenate(scores, axis=0) * scaling_factor
+            weights = jnp.exp(scores - jnp.max(scores, axis=-1, keepdims=True))
+            weights = (weights / jnp.sum(weights, axis=-1, keepdims=True)).astype(BF)
+            mixed = [
+                dot(weights[2 * CAP * j : 2 * CAP * (j + 1)], v)
+                for j, v in enumerate(heads_of(values[:, lanes], 8))
+            ]
+            mixed = jnp.concatenate(mixed, axis=1)
+            attended[:, lanes] = picked[:, lanes].astype(F32) + mixed * has_row
             return carry
 
-        lax.fori_loop(0, heads // 4, chosen_heads, 0)
+        lax.fori_loop(0, heads // 8, chosen_heads, 0)
         picked[...] = attended[...].astype(BF)
         put_capacity()
 
         def forward(group, carry):
-            for j in range(4):
-                head = group * 4 + j
-                lanes = pl.ds(pl.multiple_of(head * HD, HD), HD)
-                scores = dot(keys[:, lanes], queries[:, lanes], NT) * scaling_factor
-                weights = jnp.exp(scores - jnp.max(scores, axis=0, keepdims=True))
-                weights = weights / jnp.sum(weights, axis=0, keepdims=True)
-                probs[head] = weights
-                mixed = dot(weights.astype(BF), values[:, lanes], TN)
-                resid[:, lanes] = (cur[:, lanes].astype(F32) + mixed).astype(BF)
+            lanes = pl.ds(pl.multiple_of(group * (4 * HD), 4 * HD), 4 * HD)
+            asked, kept = heads_of(queries[:, lanes], 4), heads_of(keys[:, lanes], 4)
+            scores = [dot(k, q, NT) * scaling_factor for q, k in zip(asked, kept)]
+            weights = [jnp.exp(one - jnp.max(one, axis=0, keepdims=True)) for one in scores]
+            weights = [one / jnp.sum(one, axis=0, keepdims=True) for one in weights]
+            mixed = [
+                dot(one.astype(BF), v, TN)
+                for one, v in zip(weights, heads_of(values[:, lanes], 4))
+            ]
+            mixed = jnp.concatenate(mixed, axis=1)
+            resid[:, lanes] = (cur[:, lanes].astype(F32) + mixed).astype(BF)
+            for j, one in enumerate(weights):
+                probs[group * 4 + j] = one
             return carry
 
         def backward(group, carry):
-            for j in range(4):
-                head = group * 4 + j
-                lanes = pl.ds(pl.multiple_of(head * HD, HD), HD)
-                weights = probs[head]
-                upstream = cot[:, lanes]
-                asked = queries[:, lanes]
-                dweights = dot(values[:, lanes], upstream, NT)
-                inner = jnp.sum(dweights * weights, axis=0, keepdims=True)
-                dscores = weights * (dweights - inner) * scaling_factor
-                high = dscores.astype(BF)
-                low = (dscores - high.astype(F32)).astype(BF)
-                dkeys[:, lanes] = dot(
-                    jnp.concatenate([high, low], axis=1),
-                    jnp.concatenate([asked, asked], axis=0),
-                ).astype(BF)
-                dvalues[:, lanes] = dot(weights.astype(BF), upstream).astype(BF)
+            lanes = pl.ds(pl.multiple_of(group * (4 * HD), 4 * HD), 4 * HD)
+            weights = [probs[group * 4 + j] for j in range(4)]
+            upstream, asked = heads_of(cot[:, lanes], 4), heads_of(queries[:, lanes], 4)
+            dweights = [dot(v, g, NT) for v, g in zip(heads_of(values[:, lanes], 4), upstream)]
+            inner = [
+                jnp.sum(d * one, axis=0, keepdims=True) for d, one in zip(dweights, weights)
+            ]
+            dscores = [
+                one * (d - i) * scaling_factor for one, d, i in zip(weights, dweights, inner)
+            ]
+            high = [one.astype(BF) for one in dscores]
+            low = [(one - h.astype(F32)).astype(BF) for one, h in zip(dscores, high)]
+            dk = [
+                dot(jnp.concatenate([h, l], axis=1), jnp.concatenate([q, q], axis=0))
+                for h, l, q in zip(high, low, asked)
+            ]
+            dv = [dot(one.astype(BF), g) for one, g in zip(weights, upstream)]
+            dkeys[:, lanes] = jnp.concatenate(dk, axis=1).astype(BF)
+            dvalues[:, lanes] = jnp.concatenate(dv, axis=1).astype(BF)
             return carry
 
         def part_of(work, i, of):
@@ -596,6 +603,7 @@
 
         def hand_over():
             pass_on(0, resid, before)
+            keep(resid).start()
             loads[1].wait()
 
         drive(
@@ -629,10 +637,31 @@
         next(grad_stream)
         expert()
         drive([scatter(links, halves, parts, ret_land, ret_base), grad_stream])
-        total = gparts[x, y, z].astype(F32) + glast[...].astype(F32)
-        grad_out[...] = jnp.concatenate([total[:CAP], total[CAP:]], axis=1)
+        grad_out[...] = gparts[x, y, z].astype(F32) + glast[...].astype(F32)
         finish(resid)
+        keep(resid).wait()
         links.finish()
+
+
+def place_rows(
+    base, before, own_rows, their_rows, own_slot, their_slot, grad, layer_out, arriving, grad_out
+):
+    upper = pl.program_id(0) >= pl.num_programs(0) // 2
+    tokens, lanes = base.shape
+    row = lax.broadcasted_iota(jnp.int32, (2 * CAP, tokens), 0) - jnp.where(upper, CAP, 0)
+    for slots, rows, kept, target in (
+        (own_slot[:1, :], own_rows, base, layer_out),
+        (their_slot[:1, :], their_rows, before, arriving),
+    ):
+        chosen = jnp.where(row < 0, 0.0, (slots == row).astype(F32)).astype(BF)
+        has = dot(chosen, jnp.ones((2 * CAP, 128), BF), TN)[:, :1] > 0.5
+        for start in range(0, lanes, 256):
+            part = slice(start, start + 256)
+            moved = dot(chosen, rows[:, part], TN)
+            target[:, part] = jnp.where(has, moved, kept[:, part].astype(F32)).astype(BF)
+    total = jnp.where(upper, grad[CAP:, :], grad[:CAP, :])
+    for r in range(grad_out.shape[0]):
+        grad_out[r] = total[2 * r : 2 * r + 2]
 
 
 def local(
@@ -645,7 +674,6 @@
     ffw = expert_in.shape[2]
     half = width // 2
     heads = width // HD
-    mem = memory[0].reshape(rows * 2, 2, half).transpose(1, 0, 2).reshape(rows * 4, half)
     vmem = pl.BlockSpec(memory_space=pltpu.VMEM)
     anywhere = pl.BlockSpec(memory_space=pl.ANY)
     full = (RING, RING, 2, 2 * CAP, half)
@@ -657,21 +685,23 @@
         pltpu.VMEM((2, 2, 2, 2 * CAP, 2 * quarter), BF),
     ]
     count = 2 * GATHER_KEYS + 2 * SCATTER_KEYS + 3
-    layer_out, arriving, grad = pl.pallas_call(
+    base, before, own_rows, their_rows, their_slot, grad = pl.pallas_call(
         lambda *refs: kernel(sections, *refs),
         out_shape=(
             jax.ShapeDtypeStruct((tokens, width), BF),
             jax.ShapeDtypeStruct((tokens, width), BF),
-            jax.ShapeDtypeStruct((rows * 2, width), F32),
+            jax.ShapeDtypeStruct((2 * CAP, half), BF),
+            jax.ShapeDtypeStruct((2 * CAP, half), BF),
+            jax.ShapeDtypeStruct((8, tokens), jnp.int32),
+            jax.ShapeDtypeStruct((2 * CAP, half), F32),
         ),
         in_specs=[vmem, anywhere, anywhere, vmem, vmem, anywhere, anywhere, vmem, vmem],
-        out_specs=(vmem, vmem, vmem),
+        out_specs=(anywhere, anywhere, vmem, vmem, vmem, vmem),
         scratch_shapes=[
             pltpu.VMEM((tokens, width), BF),
             pltpu.VMEM((tokens, width), BF),
-            pltpu.VMEM((width, ffw), BF),
             pltpu.VMEM((ffw, width), BF),
-            pltpu.VMEM((tokens, width), BF),
+            pltpu.VMEM((ffw, width), BF),
             pltpu.VMEM((tokens, width), BF),
             pltpu.VMEM((tokens, width), BF),
             pltpu.VMEM(full, BF),
@@ -691,14 +721,11 @@
             pltpu.VMEM((2 * RING * RING, CAP, ffw), F32),
             pltpu.VMEM((2 * RING * RING * CAP, ffw), BF),
             pltpu.VMEM((8, tokens), jnp.int32),
-            pltpu.VMEM((8, tokens), jnp.int32),
-            pltpu.VMEM((2 * CAP, half), BF),
-            pltpu.VMEM((2 * CAP, half), BF),
             *landing,
             pltpu.VMEM((2 * CAP, half), BF),
             pltpu.VMEM((2 * CAP, half), BF),
             *landing,
-            pltpu.SemaphoreType.DMA((4,)),
+            pltpu.SemaphoreType.DMA((6,)),
             pltpu.SemaphoreType.DMA((count,)),
             pltpu.SemaphoreType.DMA((count,)),
         ],
@@ -706,17 +733,40 @@
             collective_id=0, has_side_effects=True, vmem_limit_bytes=60 * 1024 * 1024
         ),
     )(
-        mem,
+        memory[0],
         layer_in[0],
         cotangent[0],
         norm_gain,
         attn_gain,
-        expert_in[0],
+        expert_in[0].T,
         expert_out[0],
         slot_index,
         gate_prob,
     )
-    return (layer_out[None], arriving[None], grad.reshape(1, rows, 2, width))
+    steps = 4
+    lanes = width // steps
+    whole = pl.BlockSpec((tokens, lanes), lambda i: (0, i))
+    folded = pl.BlockSpec((2 * CAP, lanes), lambda i: (0, i % 2))
+    layer_out, arriving, grad_memory = pl.pallas_call(
+        place_rows,
+        grid=(steps,),
+        out_shape=(
+            jax.ShapeDtypeStruct((tokens, width), BF),
+            jax.ShapeDtypeStruct((tokens, width), BF),
+            jax.ShapeDtypeStruct((rows, 2, width), F32),
+        ),
+        in_specs=[
+            whole,
+            whole,
+            folded,
+            folded,
+            pl.BlockSpec((1, tokens), lambda i: (0, 0)),
+            pl.BlockSpec((8, tokens), lambda i: (0, 0)),
+            folded,
+        ],
+        out_specs=(whole, whole, pl.BlockSpec((rows, 2, lanes), lambda i: (0, 0, i))),
+    )(base, before, own_rows, their_rows, slot_index, their_slot, grad)
+    return (layer_out[None], arriving[None], grad_memory[None])
 
 
 def solution(mesh):

time: 133 us -> 110 us (0.83)
  local copies, waits for them, and re-layouts: 12.7 us -> 0 us
  Pallas kernels: 119 us -> 109 us
    pallas_call x1, Pallas kernels: 119 us -> 105 us  [local(): pl.pallas_call(lambda *refs: kernel(sections, *refs), out_shape=(jax.Shap...]
    unnamed x5 -> x0, local copies, waits for them, and re-layouts: 9.45 us -> none
    pallas_call x0 -> x1, Pallas kernels: none -> 4.65 us  [local(): pl.pallas_call(place_rows, grid=(steps,), out_shape=(jax.ShapeDtypeStruct...]
    reshape x1 -> x0, local copies, waits for them, and re-layouts: 1.68 us -> none  [local(): return (layer_out[None], arriving[None], grad.reshape(1, rows, 2, width))]
    another operation x2 -> x0, local copies, waits for them, and re-layouts: 1.59 us -> none  [local(): memory[0].reshape(rows * 2, 2, half).transpose(1, 0, 2)]
where the time goes in v2:
time: 110 us
  Pallas kernels  109 us (99%)
    pallas_call x1, Pallas kernels, local(): pl.pallas_call(lambda *refs: kernel(sections, *refs), out_shape=(jax.Shap...  105 us
    pallas_call x1, Pallas kernels, local(): pl.pallas_call(place_rows, grid=(steps,), out_shape=(jax.ShapeDtypeStruct...  4.65 us

profile of v2, /device:TPU:129, one launch (start us, length us, event | category | flops | bytes accessed | tf_op | source)
XLA Modules:
  0.0 110.1 jit_solution(7056076539462809663)
XLA Ops:
  0.6 104.8 %shard_map.112 = (bf16[128,5120]{1,0:T(8,128)(2,1)}, bf16[128,5120]{1,0:T(8,128)(2,1)}, bf16[16,2560]{1,0:T(8,128)(2,1)}, bf16[16,2560]{1,0:T(8,128)(2,1)}, s32[8,128]{1,0:T(8,128)}, /*index=5*/f32[16,2560]{1,0:T(8,128)}) custom-call(bf16[4,2,5120]{2,1,0:T(2,128)(2,1)} %bitcast.14, bf16[128,5120]{1,0:T(8,128)(2,1)} %bitcast.12, bf16[128,5120]{1,0:T(8,128)(2,1)} %bitcast.13, ...), custom_call_target="tpu_custom_call" | custom-call | tf_op jit(solution)/shard_map/pallas_call | solution.py:688
  105.4 4.7 %shard_map.113 = (bf16[128,5120]{1,0:T(8,128)(2,1)}, bf16[128,5120]{1,0:T(8,128)(2,1)}, f32[4,2,5120]{2,1,0:T(2,128)}) custom-call(bf16[128,5120]{1,0:T(8,128)(2,1)} %get-tuple-element.12.base, bf16[128,5120]{1,0:T(8,128)(2,1)} %get-tuple-element.13.before, bf16[16,2560]{1,0:T(8,128)(2,1)} %get-tuple-element.14.own_rows, ...), custom_call_target="tpu_custom_call" | custom-call | tf_op jit(solution)/shard_map/pallas_call | solution.py:750

commit v3 on v2

--- a/solution.py
+++ b/solution.py
@@ -49,6 +49,9 @@
         self.started = []
 
 
+GROUP = ((2, 0), (2, 1), (1, 0), (3, 0), (1, 1), (3, 1), (0, 1))
+
+
 class Half:
     def __init__(self, links, first, lane, width):
         self.links, self.first, self.lane, self.width = links, first, lane, width
@@ -60,90 +63,84 @@
             return buf.at[u, v, :, :, lanes]
         return buf.at[v, u, :, :, lanes]
 
-    def device(self, u, v):
+    def one(self, buf, u, v, z, low=0, size=None):
+        lanes = pl.ds(self.lane + low, self.width if size is None else size)
+        if self.first == "x":
+            return buf.at[u, v, z, :, lanes]
+        return buf.at[v, u, z, :, lanes]
+
+    def device(self, u, v, z=None):
         x, y = (u, v) if self.first == "x" else (v, u)
-        return (self.links.section, x * (RING * 2) + y * 2 + self.links.z)
+        z = self.links.z if z is None else z
+        return (self.links.section, x * (RING * 2) + y * 2 + z)
 
 
 def step(i, by):
     return lax.rem(i + by + RING, RING)
 
 
-GATHER_KEYS = 41
-SCATTER_KEYS = 41
+GATHER_KEYS = 78
+SCATTER_KEYS = 46
+PIECES = 1
+TURNS = ((0, 1), (1, -1))
 
 
 def gather(links, halves, buf, base):
-    x, y, z = links.x, links.y, links.z
-    pair = (links.section, x * (RING * 2) + y * 2 + (1 - z))
-    links.put(base, buf.at[x, y, z], buf.at[x, y, z], pair)
+    z = links.z
+    keyed = [(half, base + 39 * i) for i, half in enumerate(halves)]
+
+    def source(half, slot):
+        if slot == 7:
+            return half.u, z
+        du, dz = GROUP[slot]
+        return step(half.u, -du), (z + dz) % 2
+
+    def spread(half, key, slot):
+        u, zz = source(half, slot)
+        part = half.one(buf, u, half.v, zz)
+        for d, turn in TURNS:
+            links.put(key + 7 + slot * 4 + d, part, part, half.device(half.u, step(half.v, turn)))
+
+    def relay(slot):
+        for half, key in keyed:
+            q = half.width // 2
+            u, zz = source(half, slot)
+            k = key + 7 + slot * 4
+            for d, turn in TURNS:
+                left = step(half.v, -turn)
+                links.got(k + d, half.one(buf, u, left, zz), half.device(half.u, left))
+                part = half.one(buf, u, left, zz, d * q, q)
+                links.put(k + 2 + d, part, part, half.device(half.u, step(half.v, turn)))
+
+    for i, (du, dz) in enumerate(GROUP):
+        for half, key in keyed:
+            part = half.one(buf, half.u, half.v, z)
+            links.put(key + i, part, part, half.device(step(half.u, du), half.v, (z + dz) % 2))
+    for half, key in keyed:
+        spread(half, key, 7)
     yield
-    links.got(base, buf.at[x, y, 1 - z], pair)
-
-    def spread(half, key, slot, u):
-        part = half.at(buf, u, half.v)
-        for turn in (1, -1):
-            links.put(
-                key + 4 + slot * 4 + (turn < 0),
-                part,
-                part,
-                half.device(half.u, step(half.v, turn)),
-            )
-
-    def relay(half, key, slot, u):
-        q = half.width // 2
-        for turn in (1, -1):
-            left = step(half.v, -turn)
-            k = key + 4 + slot * 4 + (turn < 0)
-            links.got(k, half.at(buf, u, left), half.device(half.u, left))
-            part = half.at(buf, u, left, 0 if turn > 0 else q, q)
-            links.put(k + 2, part, part, half.device(half.u, step(half.v, turn)))
-
-    keyed = [(half, base + 1 + 20 * i) for i, half in enumerate(halves)]
-    for half, key in keyed:
-        part = half.at(buf, half.u, half.v)
-        for turn in (1, -1):
-            links.put(key + (turn < 0), part, part, half.device(step(half.u, turn), half.v))
-    for half, key in keyed:
-        spread(half, key, 0, half.u)
+    order = (6, 2, 3, 4, 5, 0, 1)
+    for n, slot in enumerate(order):
+        for half, key in keyed:
+            u, zz = source(half, slot)
+            links.got(key + slot, half.one(buf, u, half.v, zz), half.device(u, half.v, zz))
+            spread(half, key, slot)
+        if n == 3:
+            relay(7)
+            yield
     yield
-    for half, key in keyed:
-        q = half.width // 2
-        for slot, turn in ((1, 1), (2, -1)):
-            left = step(half.u, -turn)
-            links.got(key + (turn < 0), half.at(buf, left, half.v), half.device(left, half.v))
-            part = half.at(buf, left, half.v, 0 if turn > 0 else q, q)
-            links.put(key + 2 + (turn < 0), part, part, half.device(step(half.u, turn), half.v))
-            spread(half, key, slot, left)
-    yield
-    for half, key in keyed:
-        relay(half, key, 0, half.u)
-    yield
-    for half, key in keyed:
-        q = half.width // 2
-        far = step(half.u, 2)
-        for turn in (1, -1):
-            part = half.at(buf, far, half.v, 0 if turn > 0 else q, q)
-            links.got(key + 2 + (turn < 0), part, half.device(step(half.u, -turn), half.v))
-        spread(half, key, 3, far)
-    yield
-    for half, key in keyed:
-        relay(half, key, 1, step(half.u, -1))
-        relay(half, key, 2, step(half.u, 1))
-    yield
-    for half, key in keyed:
-        relay(half, key, 3, step(half.u, 2))
-    yield
-    for half, key in keyed:
-        q = half.width // 2
-        for slot, by in ((0, 0), (1, -1), (2, 1), (3, 2)):
-            for turn in (1, -1):
-                part = half.at(
-                    buf, step(half.u, by), step(half.v, 2), 0 if turn > 0 else q, q
-                )
+    for n, slot in enumerate(order):
+        relay(slot)
+        if n in (3, 6):
+            yield
+    for slot in (7,) + order:
+        for half, key in keyed:
+            q = half.width // 2
+            u, zz = source(half, slot)
+            for d, turn in TURNS:
                 links.got(
-                    key + 4 + slot * 4 + 2 + (turn < 0),
-                    part,
+                    key + 7 + slot * 4 + 2 + d,
+                    half.one(buf, u, step(half.v, 2), zz, d * q, q),
                     half.device(half.u, step(half.v, -turn)),
                 )
 
@@ -156,87 +153,73 @@
 
 
 def scatter(links, halves, buf, land, base):
-    passing2, whole2, passing1, whole1, last = land
-    x, y, z = links.x, links.y, links.z
+    passing, whole, last = land
+    z = links.z
     order = ((0, 2), (1, -1), (2, 1), (3, 0))
-    keyed = [(i, half, base + 1 + 20 * i) for i, half in enumerate(halves)]
+    keyed = [(i, half, base + 23 * i) for i, half in enumerate(halves)]
     for slot, by in order:
         for i, half, key in keyed:
             q = half.width // 2
-            for turn in (1, -1):
-                d = int(turn < 0)
+            for d, turn in TURNS:
                 links.put(
                     key + slot * 4 + d,
                     half.at(buf, step(half.u, by), step(half.v, 2), d * q, q),
-                    passing2.at[i, slot, d],
+                    passing.at[i, slot, d],
                     half.device(half.u, step(half.v, turn)),
                 )
     yield
     for slot, by in order:
         for i, half, key in keyed:
             q = half.width // 2
-            for turn in (1, -1):
-                d = int(turn < 0)
+            for d, turn in TURNS:
                 to = step(half.v, turn)
                 links.got(
                     key + slot * 4 + d,
-                    passing2.at[i, slot, d],
+                    passing.at[i, slot, d],
                     half.device(half.u, step(half.v, -turn)),
                 )
-                add_into(
-                    half.at(buf, step(half.u, by), to, d * q, q), passing2.at[i, slot, d]
-                )
+                add_into(half.at(buf, step(half.u, by), to, d * q, q), passing.at[i, slot, d])
                 links.put(
                     key + slot * 4 + 2 + d,
                     half.at(buf, step(half.u, by), to),
-                    whole2.at[i, slot, d],
+                    whole.at[i, slot, d],
                     half.device(half.u, to),
                 )
         yield
     for slot, by in order:
         for i, half, key in keyed:
-            q = half.width // 2
-            for d, turn in ((0, 1), (1, -1)):
+            for d, turn in TURNS:
                 links.got(
                     key + slot * 4 + 2 + d,
-                    whole2.at[i, slot, d],
+                    whole.at[i, slot, d],
                     half.device(half.u, step(half.v, -turn)),
                 )
             add_into(
                 half.at(buf, step(half.u, by), half.v),
-                whole2.at[i, slot, 0],
-                whole2.at[i, slot, 1],
+                whole.at[i, slot, 0],
+                whole.at[i, slot, 1],
             )
-            if by == 2:
-                for d, turn in ((0, 1), (1, -1)):
+            for j, (du, dz) in enumerate(GROUP):
+                if du == by % RING:
+                    u, zz = step(half.u, du), (z + dz) % 2
                     links.put(
-                        key + 16 + d,
-                        half.at(buf, step(half.u, 2), half.v, d * q, q),
-                        passing1.at[i, d],
-                        half.device(step(half.u, turn), half.v),
-                    )
-            if by == 1:
-                for d, turn in ((0, 1), (1, -1)):
-                    to = step(half.u, turn)
-                    links.got(
-                        key + 16 + d, passing1.at[i, d], half.device(step(half.u, -turn), half.v)
-                    )
-                    add_into(half.at(buf, to, half.v, d * q, q), passing1.at[i, d])
-                    links.put(
-                        key + 18 + d,
-                        half.at(buf, to, half.v),
-                        whole1.at[i, d],
-                        half.device(to, half.v),
+                        key + 16 + j,
+                        half.one(buf, u, half.v, zz),
+                        last.at[i, j],
+                        half.device(u, half.v, zz),
                     )
         yield
     for i, half, key in keyed:
-        for d, turn in ((0, 1), (1, -1)):
-            links.got(key + 18 + d, whole1.at[i, d], half.device(step(half.u, -turn), half.v))
-        add_into(half.at(buf, half.u, half.v), whole1.at[i, 0], whole1.at[i, 1])
-    pair = (links.section, x * (RING * 2) + y * 2 + (1 - z))
-    links.put(base, buf.at[x, y, 1 - z], last, pair)
-    yield
-    links.got(base, last, pair)
+        for j, (du, dz) in enumerate(GROUP):
+            u, zz = step(half.u, -du), (z + dz) % 2
+            links.got(key + 16 + j, last.at[i, j], half.device(u, half.v, zz))
+
+
+def scattered(buf, place, land):
+    last = land[2]
+    total = buf[place].astype(F32)
+    others = [jnp.sum(last[i].astype(F32), axis=0) for i in range(2)]
+    return total + jnp.concatenate(others, axis=1)
 
 
 def drive(streams, tasks=()):
@@ -296,13 +279,9 @@
     land_a,
     land_b,
     land_c,
-    land_d,
-    land_e,
-    glast,
     gland_a,
     gland_b,
     gland_c,
-    gland_d,
     load_sem,
     send_sem,
     recv_sem,
@@ -338,13 +317,9 @@
         return (section, xx * (RING * 2) + yy * 2 + zz)
 
     barrier = pltpu.get_barrier_semaphore()
-    for peer in (
-        device(x, y, 1 - z),
-        device(step(x, 1), y, z),
-        device(step(x, -1), y, z),
-        device(x, step(y, 1), z),
-        device(x, step(y, -1), z),
-    ):
+    peers = [device(step(x, dx), y, (z + dz) % 2) for dx in range(RING) for dz in range(2) if dx or dz]
+    peers += [device(x, step(y, dy), (z + dz) % 2) for dy in range(1, RING) for dz in range(2)]
+    for peer in peers:
         pl.semaphore_signal(barrier, inc=1, device_id=peer, device_id_type=MESH)
 
     @pl.when(section > 0)
@@ -360,7 +335,7 @@
         )
 
     ends = jnp.where(section > 0, 1, 0) + jnp.where(section < sections - 1, 1, 0)
-    pl.semaphore_wait(barrier, 5 + ends)
+    pl.semaphore_wait(barrier, len(peers) + ends)
 
     def pass_copy(key, src, dst):
         return links.copy(pass_base + key, src, dst, (section + 1, place))
@@ -379,6 +354,12 @@
         @pl.when(section > 0)
         def _():
             links.copy(pass_base + key, dst, dst, (section - 1, place)).wait_recv()
+
+    def piece(ref, i):
+        return ref.at[:, pl.ds(i * (width // PIECES), width // PIECES)]
+
+    def pass_piece(base, i):
+        return lambda: pass_on(2 + i, piece(base, i), piece(before, i))
 
     slots = slot_ref[...]
     rows16 = lax.broadcasted_iota(jnp.int32, (2 * CAP, tokens), 0)
@@ -430,23 +411,26 @@
 
         lax.fori_loop(0, half_width // 256, out, 0)
 
-    ret_land = (land_a, land_b, land_c, land_d, land_e)
+    ret_land = (land_a, land_b, land_c)
+    grad_land = (gland_a, gland_b, gland_c)
 
     def finish(base):
-        returned = parts[x, y, z].astype(F32) + land_e[...].astype(F32)
+        returned = scattered(parts, (x, y, z), ret_land)
         gates = jnp.sum(
             jnp.where(slots == rows16[:CAP], gate_ref[...], 0.0), axis=-1, keepdims=True
         )
         gates = jnp.concatenate([gates, gates], axis=0)
         own_rows[...] = (fold(picked[...].astype(F32)) + gates * returned).astype(BF)
-        pass_on(2, own_rows, their_rows)
-        pass_got(0, before)
+        pass_on(0, own_rows, their_rows)
+        for i in range(PIECES):
+            pass_got(2 + i, piece(before, i))
         pass_got(1, their_slot)
-        pass_got(2, their_rows)
-
-        pass_sent(0, base, before)
+        pass_got(0, their_rows)
+
+        for i in range(PIECES):
+            pass_sent(2 + i, piece(base, i), piece(before, i))
         pass_sent(1, own_slot, their_slot)
-        pass_sent(2, own_rows, their_rows)
+        pass_sent(0, own_rows, their_rows)
 
     own_slot[...] = jnp.broadcast_to(slots, own_slot.shape)
     nothing = pltpu.make_async_copy(resid, before, load_sem.at[5])
@@ -461,7 +445,6 @@
         put_capacity()
         stream = gather(links, halves, gcap, cap_base)
         next(stream)
-        pass_on(0, cur, before)
         pass_on(1, own_slot, their_slot)
         keep(cur).start()
 
@@ -475,6 +458,7 @@
         drive([stream])
         loads[1].wait()
         expert()
+        pass_piece(cur, 0)()
         drive([scatter(links, halves, parts, ret_land, ret_base)])
         grad_out[...] = jnp.zeros_like(grad_out)
         finish(cur)
@@ -601,15 +585,22 @@
 
             return task
 
-        def hand_over():
-            pass_on(0, resid, before)
+        def forward_piece(i):
+            def task():
+                of = heads // 4 // PIECES
+                lax.fori_loop(i * of, (i + 1) * of, forward, 0)
+                pass_piece(resid, i)()
+
+            return task
+
+        def keep_rows():
             keep(resid).start()
             loads[1].wait()
 
         drive(
             [gather(links, halves, gcap, cap_base)],
-            [part_of(forward, i, 4) for i in range(4)]
-            + [hand_over]
+            [forward_piece(i) for i in range(PIECES)]
+            + [keep_rows]
             + [part_of(backward, i, 4) for i in range(4)],
         )
 
@@ -632,12 +623,12 @@
             lax.fori_loop(0, half_width // 256, sort_out, 0)
 
         grad_stream = scatter(
-            links, halves, gparts, (gland_a, gland_b, gland_c, gland_d, glast), grad_base
+            links, halves, gparts, grad_land, grad_base
         )
         next(grad_stream)
         expert()
         drive([scatter(links, halves, parts, ret_land, ret_base), grad_stream])
-        grad_out[...] = gparts[x, y, z].astype(F32) + glast[...].astype(F32)
+        grad_out[...] = scattered(gparts, (x, y, z), grad_land)
         finish(resid)
         keep(resid).wait()
         links.finish()
@@ -681,10 +672,9 @@
     landing = [
         pltpu.VMEM((2, RING, 2, 2, 2 * CAP, quarter), BF),
         pltpu.VMEM((2, RING, 2, 2, 2 * CAP, 2 * quarter), BF),
-        pltpu.VMEM((2, 2, 2, 2 * CAP, quarter), BF),
-        pltpu.VMEM((2, 2, 2, 2 * CAP, 2 * quarter), BF),
+        pltpu.VMEM((2, len(GROUP), 2 * CAP, 2 * quarter), BF),
     ]
-    count = 2 * GATHER_KEYS + 2 * SCATTER_KEYS + 3
+    count = 2 * GATHER_KEYS + 2 * SCATTER_KEYS + PIECES + 2
     base, before, own_rows, their_rows, their_slot, grad = pl.pallas_call(
         lambda *refs: kernel(sections, *refs),
         out_shape=(
@@ -722,8 +712,6 @@
             pltpu.VMEM((2 * RING * RING * CAP, ffw), BF),
             pltpu.VMEM((8, tokens), jnp.int32),
             *landing,
-            pltpu.VMEM((2 * CAP, half), BF),
-            pltpu.VMEM((2 * CAP, half), BF),
             *landing,
             pltpu.SemaphoreType.DMA((6,)),
             pltpu.SemaphoreType.DMA((count,)),

time: 110 us -> 103 us (0.936)
  Pallas kernels: 109 us -> 102 us
    pallas_call x1, Pallas kernels: 105 us -> 97.7 us  [local(): pl.pallas_call(lambda *refs: kernel(sections, *refs), out_shape=(jax.Shap...]
where the time goes in v3:
time: 103 us
  Pallas kernels  102 us (99%)
    pallas_call x1, Pallas kernels, local(): pl.pallas_call(lambda *refs: kernel(sections, *refs), out_shape=(jax.Shap...  97.7 us
    pallas_call x1, Pallas kernels, local(): pl.pallas_call(place_rows, grid=(steps,), out_shape=(jax.ShapeDtypeStruct...  4.65 us

profile of v3, /device:TPU:129, one launch (start us, length us, event | category | flops | bytes accessed | tf_op | source)
XLA Modules:
  0.0 103.0 jit_solution(4493017871349471220)
XLA Ops:
  0.6 97.7 %shard_map.112 = (bf16[128,5120]{1,0:T(8,128)(2,1)}, bf16[128,5120]{1,0:T(8,128)(2,1)}, bf16[16,2560]{1,0:T(8,128)(2,1)}, bf16[16,2560]{1,0:T(8,128)(2,1)}, s32[8,128]{1,0:T(8,128)}, /*index=5*/f32[16,2560]{1,0:T(8,128)}) custom-call(bf16[4,2,5120]{2,1,0:T(2,128)(2,1)} %bitcast.14, bf16[128,5120]{1,0:T(8,128)(2,1)} %bitcast.12, bf16[128,5120]{1,0:T(8,128)(2,1)} %bitcast.13, ...), custom_call_target="tpu_custom_call" | custom-call | tf_op jit(solution)/shard_map/pallas_call | solution.py:678
  98.3 4.7 %shard_map.113 = (bf16[128,5120]{1,0:T(8,128)(2,1)}, bf16[128,5120]{1,0:T(8,128)(2,1)}, f32[4,2,5120]{2,1,0:T(2,128)}) custom-call(bf16[128,5120]{1,0:T(8,128)(2,1)} %get-tuple-element.12.base, bf16[128,5120]{1,0:T(8,128)(2,1)} %get-tuple-element.13.before, bf16[16,2560]{1,0:T(8,128)(2,1)} %get-tuple-element.14.own_rows, ...), custom_call_target="tpu_custom_call" | custom-call | tf_op jit(solution)/shard_map/pallas_call | solution.py:738

commit v4 on v3

--- a/solution.py
+++ b/solution.py
@@ -388,17 +388,15 @@
 
         def into(k, carry):
             lanes = pl.ds(pl.multiple_of(k * 256, 256), 256)
-            block = gcap[:, :, :, :, lanes].reshape(-1, 256)
+            block = gcap[:, :, :, :, lanes].reshape(-1, 2 * CAP, 256).astype(F32)
+            low = block[:, :CAP].reshape(-1, 256).astype(BF)
+            high = block[:, CAP:].reshape(-1, 256).astype(BF)
             high_lanes = pl.ds(pl.multiple_of(half_width + k * 256, 256), 256)
-            low = dot(block, win[:, lanes], NT)
-            high = dot(block, win[:, high_lanes], NT)
-            low = low.reshape(-1, 2 * CAP, ffw)[:, :CAP]
-            high = high.reshape(-1, 2 * CAP, ffw)[:, CAP:]
-            hacc[...] += low + high
+            hacc[...] += dot(win[:, lanes], low, NT) + dot(win[:, high_lanes], high, NT)
             return carry
 
         lax.fori_loop(0, half_width // 256, into, 0)
-        hidden[...] = jax.nn.gelu(hacc[...].reshape(-1, ffw)).astype(BF)
+        hidden[...] = jax.nn.gelu(hacc[...]).T.astype(BF)
 
         def out(k, carry):
             lanes = pl.ds(pl.multiple_of(k * 256, 256), 256)
@@ -502,40 +500,43 @@
             [lambda: pass_on(1, own_slot, their_slot), make_perm, make_queries, pick_rows],
         )
 
-        for c in range(2):
-
-            def sort_in(i, carry, c=c):
-                lanes = pl.ds(pl.multiple_of(i * 256, 256), 256)
-                high = pl.ds(pl.multiple_of(half_width + i * 256, 256), 256)
-                block = gkv[2 * c : 2 * c + 2, :, :, :, lanes].reshape(256, 256)
-                block = dot(perm[...], block).astype(BF)
-                keys[64 * c : 64 * c + 64, lanes] = block[:64]
-                values[64 * c : 64 * c + 64, lanes] = block[64:128]
-                keys[64 * c : 64 * c + 64, high] = block[128:192]
-                values[64 * c : 64 * c + 64, high] = block[192:]
-                return carry
-
-            lax.fori_loop(0, half_width // 256, sort_in, 0)
+        def sort_in(i, carry):
+            lanes = pl.ds(pl.multiple_of(i * 256, 256), 256)
+            high = pl.ds(pl.multiple_of(half_width + i * 256, 256), 256)
+            blocks = [gkv[2 * c : 2 * c + 2, :, :, :, lanes].reshape(256, 256) for c in range(2)]
+            blocks = [dot(perm[...], block).astype(BF) for block in blocks]
+            for start, target, place in (
+                (0, keys, lanes),
+                (64, values, lanes),
+                (128, keys, high),
+                (192, values, high),
+            ):
+                target[:, place] = jnp.concatenate(
+                    [block[start : start + 64] for block in blocks], axis=0
+                )
+            return carry
+
+        lax.fori_loop(0, half_width // 256, sort_in, 0)
 
         def heads_of(block, count):
             return [block[:, j * HD : (j + 1) * HD] for j in range(count)]
 
         def chosen_heads(group, carry):
-            lanes = pl.ds(pl.multiple_of(group * (8 * HD), 8 * HD), 8 * HD)
-            asked, kept = heads_of(pickedq[:, lanes], 8), heads_of(keys[:, lanes], 8)
+            lanes = pl.ds(pl.multiple_of(group * (20 * HD), 20 * HD), 20 * HD)
+            asked, kept = heads_of(pickedq[:, lanes], 20), heads_of(keys[:, lanes], 20)
             scores = [dot(q, k, NT) for q, k in zip(asked, kept)]
             scores = jnp.concatenate(scores, axis=0) * scaling_factor
             weights = jnp.exp(scores - jnp.max(scores, axis=-1, keepdims=True))
             weights = (weights / jnp.sum(weights, axis=-1, keepdims=True)).astype(BF)
             mixed = [
                 dot(weights[2 * CAP * j : 2 * CAP * (j + 1)], v)
-                for j, v in enumerate(heads_of(values[:, lanes], 8))
+                for j, v in enumerate(heads_of(values[:, lanes], 20))
             ]
             mixed = jnp.concatenate(mixed, axis=1)
             attended[:, lanes] = picked[:, lanes].astype(F32) + mixed * has_row
             return carry
 
-        lax.fori_loop(0, heads // 8, chosen_heads, 0)
+        lax.fori_loop(0, heads // 20, chosen_heads, 0)
         picked[...] = attended[...].astype(BF)
         put_capacity()
 
@@ -604,23 +605,21 @@
             + [part_of(backward, i, 4) for i in range(4)],
         )
 
-        for c in range(2):
-
-            def sort_out(i, carry, c=c):
-                lanes = pl.ds(pl.multiple_of(i * 256, 256), 256)
-                high = pl.ds(pl.multiple_of(half_width + i * 256, 256), 256)
-                rows = slice(64 * c, 64 * c + 64)
-                block = jnp.concatenate(
-                    [dkeys[rows, lanes], dvalues[rows, lanes], dkeys[rows, high], dvalues[rows, high]],
-                    axis=0,
-                )
-                block = dot(perm_t[...], block).astype(BF)
-                gparts[2 * c : 2 * c + 2, :, :, :, lanes] = block.reshape(
-                    2, RING, 2, 2 * CAP, 256
-                )
-                return carry
-
-            lax.fori_loop(0, half_width // 256, sort_out, 0)
+        def sort_out(i, carry):
+            lanes = pl.ds(pl.multiple_of(i * 256, 256), 256)
+            high = pl.ds(pl.multiple_of(half_width + i * 256, 256), 256)
+            taken = [dkeys[:, lanes], dvalues[:, lanes], dkeys[:, high], dvalues[:, high]]
+            blocks = [
+                jnp.concatenate([one[64 * c : 64 * c + 64] for one in taken], axis=0)
+                for c in range(2)
+            ]
+            blocks = [dot(perm_t[...], block).astype(BF) for block in blocks]
+            gparts[:, :, :, :, lanes] = jnp.concatenate(blocks, axis=0).reshape(
+                RING, RING, 2, 2 * CAP, 256
+            )
+            return carry
+
+        lax.fori_loop(0, half_width // 256, sort_out, 0)
 
         grad_stream = scatter(
             links, halves, gparts, grad_land, grad_base
@@ -645,11 +644,12 @@
         (their_slot[:1, :], their_rows, before, arriving),
     ):
         chosen = jnp.where(row < 0, 0.0, (slots == row).astype(F32)).astype(BF)
-        has = dot(chosen, jnp.ones((2 * CAP, 128), BF), TN)[:, :1] > 0.5
+        turned = chosen.astype(F32).T.astype(BF)
+        free = (1.0 - jnp.sum(turned.astype(F32), axis=-1, keepdims=True)).astype(BF)
         for start in range(0, lanes, 256):
             part = slice(start, start + 256)
-            moved = dot(chosen, rows[:, part], TN)
-            target[:, part] = jnp.where(has, moved, kept[:, part].astype(F32)).astype(BF)
+            moved = dot(turned, rows[:, part]).astype(BF)
+            target[:, part] = moved + kept[:, part] * free
     total = jnp.where(upper, grad[CAP:, :], grad[:CAP, :])
     for r in range(grad_out.shape[0]):
         grad_out[r] = total[2 * r : 2 * r + 2]
@@ -708,7 +708,7 @@
             pltpu.VMEM((2 * CAP, width), F32),
             pltpu.VMEM((256, 256), BF),
             pltpu.VMEM((256, 256), BF),
-            pltpu.VMEM((2 * RING * RING, CAP, ffw), F32),
+            pltpu.VMEM((ffw, 2 * RING * RING * CAP), F32),
             pltpu.VMEM((2 * RING * RING * CAP, ffw), BF),
             pltpu.VMEM((8, tokens), jnp.int32),
             *landing,
@@ -731,10 +731,10 @@
         slot_index,
         gate_prob,
     )
-    steps = 4
+    steps = 2
     lanes = width // steps
     whole = pl.BlockSpec((tokens, lanes), lambda i: (0, i))
-    folded = pl.BlockSpec((2 * CAP, lanes), lambda i: (0, i % 2))
+    folded = pl.BlockSpec((2 * CAP, lanes), lambda i: (0, i % (steps // 2)))
     layer_out, arriving, grad_memory = pl.pallas_call(
         place_rows,
         grid=(steps,),

time: 103 us -> 97.1 us (0.943)
  Pallas kernels: 102 us -> 96.3 us
    pallas_call x1, Pallas kernels: 97.7 us -> 92.8 us  [local(): pl.pallas_call(lambda *refs: kernel(sections, *refs), out_shape=(jax.Shap...]
    pallas_call x1, Pallas kernels: 4.65 us -> 3.48 us  [local(): pl.pallas_call(place_rows, grid=(steps,), out_shape=(jax.ShapeDtypeStruct...]
where the time goes in v4:
time: 97.1 us; the launch traced here: 96.9 us
  Pallas kernels  96.3 us (99%)
    pallas_call x1, Pallas kernels, local(): pl.pallas_call(lambda *refs: kernel(sections, *refs), out_shape=(jax.Shap...  92.8 us
    pallas_call x1, Pallas kernels, local(): pl.pallas_call(place_rows, grid=(steps,), out_shape=(jax.ShapeDtypeStruct...  3.48 us

profile of v4, /device:TPU:129, one launch (start us, length us, event | category | flops | bytes accessed | tf_op | source)
XLA Modules:
  0.0 96.9 jit_solution(2883984955462503253)
XLA Ops:
  0.6 92.8 %shard_map.112 = (bf16[128,5120]{1,0:T(8,128)(2,1)}, bf16[128,5120]{1,0:T(8,128)(2,1)}, bf16[16,2560]{1,0:T(8,128)(2,1)}, bf16[16,2560]{1,0:T(8,128)(2,1)}, s32[8,128]{1,0:T(8,128)}, /*index=5*/f32[16,2560]{1,0:T(8,128)}) custom-call(bf16[4,2,5120]{2,1,0:T(2,128)(2,1)} %bitcast.14, bf16[128,5120]{1,0:T(8,128)(2,1)} %bitcast.12, bf16[128,5120]{1,0:T(8,128)(2,1)} %bitcast.13, ...), custom_call_target="tpu_custom_call" | custom-call | tf_op jit(solution)/shard_map/pallas_call | solution.py:678
  93.5 3.5 %shard_map.113 = (bf16[128,5120]{1,0:T(8,128)(2,1)}, bf16[128,5120]{1,0:T(8,128)(2,1)}, f32[4,2,5120]{2,1,0:T(2,128)}) custom-call(bf16[128,5120]{1,0:T(8,128)(2,1)} %get-tuple-element.12.base, bf16[128,5120]{1,0:T(8,128)(2,1)} %get-tuple-element.13.before, bf16[16,2560]{1,0:T(8,128)(2,1)} %get-tuple-element.14.own_rows, ...), custom_call_target="tpu_custom_call" | custom-call | tf_op jit(solution)/shard_map/pallas_call | solution.py:738

commit v5 on v4

--- a/solution.py
+++ b/solution.py
@@ -387,27 +387,27 @@
         hacc[...] = jnp.zeros_like(hacc)
 
         def into(k, carry):
-            lanes = pl.ds(pl.multiple_of(k * 256, 256), 256)
-            block = gcap[:, :, :, :, lanes].reshape(-1, 2 * CAP, 256).astype(F32)
-            low = block[:, :CAP].reshape(-1, 256).astype(BF)
-            high = block[:, CAP:].reshape(-1, 256).astype(BF)
-            high_lanes = pl.ds(pl.multiple_of(half_width + k * 256, 256), 256)
+            lanes = pl.ds(pl.multiple_of(k * 512, 512), 512)
+            block = gcap[:, :, :, :, lanes].reshape(-1, 2 * CAP, 512).astype(F32)
+            low = block[:, :CAP].reshape(-1, 512).astype(BF)
+            high = block[:, CAP:].reshape(-1, 512).astype(BF)
+            high_lanes = pl.ds(pl.multiple_of(half_width + k * 512, 512), 512)
             hacc[...] += dot(win[:, lanes], low, NT) + dot(win[:, high_lanes], high, NT)
             return carry
 
-        lax.fori_loop(0, half_width // 256, into, 0)
+        lax.fori_loop(0, half_width // 512, into, 0)
         hidden[...] = jax.nn.gelu(hacc[...]).T.astype(BF)
 
         def out(k, carry):
-            lanes = pl.ds(pl.multiple_of(k * 256, 256), 256)
-            high_lanes = pl.ds(pl.multiple_of(half_width + k * 256, 256), 256)
-            low = dot(hidden[...], wout[:, lanes]).reshape(-1, CAP, 256)
-            high = dot(hidden[...], wout[:, high_lanes]).reshape(-1, CAP, 256)
+            lanes = pl.ds(pl.multiple_of(k * 512, 512), 512)
+            high_lanes = pl.ds(pl.multiple_of(half_width + k * 512, 512), 512)
+            low = dot(hidden[...], wout[:, lanes]).reshape(-1, CAP, 512)
+            high = dot(hidden[...], wout[:, high_lanes]).reshape(-1, CAP, 512)
             block = jnp.concatenate([low, high], axis=1).astype(BF)
-            parts[:, :, :, :, lanes] = block.reshape(RING, RING, 2, 2 * CAP, 256)
+            parts[:, :, :, :, lanes] = block.reshape(RING, RING, 2, 2 * CAP, 512)
             return carry
 
-        lax.fori_loop(0, half_width // 256, out, 0)
+        lax.fori_loop(0, half_width // 512, out, 0)
 
     ret_land = (land_a, land_b, land_c)
     grad_land = (gland_a, gland_b, gland_c)
@@ -501,9 +501,9 @@
         )
 
         def sort_in(i, carry):
-            lanes = pl.ds(pl.multiple_of(i * 256, 256), 256)
-            high = pl.ds(pl.multiple_of(half_width + i * 256, 256), 256)
-            blocks = [gkv[2 * c : 2 * c + 2, :, :, :, lanes].reshape(256, 256) for c in range(2)]
+            lanes = pl.ds(pl.multiple_of(i * 512, 512), 512)
+            high = pl.ds(pl.multiple_of(half_width + i * 512, 512), 512)
+            blocks = [gkv[2 * c : 2 * c + 2, :, :, :, lanes].reshape(256, 512) for c in range(2)]
             blocks = [dot(perm[...], block).astype(BF) for block in blocks]
             for start, target, place in (
                 (0, keys, lanes),
@@ -516,7 +516,7 @@
                 )
             return carry
 
-        lax.fori_loop(0, half_width // 256, sort_in, 0)
+        lax.fori_loop(0, half_width // 512, sort_in, 0)
 
         def heads_of(block, count):
             return [block[:, j * HD : (j + 1) * HD] for j in range(count)]
@@ -541,26 +541,26 @@
         put_capacity()
 
         def forward(group, carry):
-            lanes = pl.ds(pl.multiple_of(group * (4 * HD), 4 * HD), 4 * HD)
-            asked, kept = heads_of(queries[:, lanes], 4), heads_of(keys[:, lanes], 4)
+            lanes = pl.ds(pl.multiple_of(group * (8 * HD), 8 * HD), 8 * HD)
+            asked, kept = heads_of(queries[:, lanes], 8), heads_of(keys[:, lanes], 8)
             scores = [dot(k, q, NT) * scaling_factor for q, k in zip(asked, kept)]
             weights = [jnp.exp(one - jnp.max(one, axis=0, keepdims=True)) for one in scores]
             weights = [one / jnp.sum(one, axis=0, keepdims=True) for one in weights]
             mixed = [
                 dot(one.astype(BF), v, TN)
-                for one, v in zip(weights, heads_of(values[:, lanes], 4))
+                for one, v in zip(weights, heads_of(values[:, lanes], 8))
             ]
             mixed = jnp.concatenate(mixed, axis=1)
             resid[:, lanes] = (cur[:, lanes].astype(F32) + mixed).astype(BF)
             for j, one in enumerate(weights):
-                probs[group * 4 + j] = one
+                probs[group * 8 + j] = one
             return carry
 
         def backward(group, carry):
-            lanes = pl.ds(pl.multiple_of(group * (4 * HD), 4 * HD), 4 * HD)
-            weights = [probs[group * 4 + j] for j in range(4)]
-            upstream, asked = heads_of(cot[:, lanes], 4), heads_of(queries[:, lanes], 4)
-            dweights = [dot(v, g, NT) for v, g in zip(heads_of(values[:, lanes], 4), upstream)]
+            lanes = pl.ds(pl.multiple_of(group * (8 * HD), 8 * HD), 8 * HD)
+            weights = [probs[group * 8 + j] for j in range(8)]
+            upstream, asked = heads_of(cot[:, lanes], 8), heads_of(queries[:, lanes], 8)
+            dweights = [dot(v, g, NT) for v, g in zip(heads_of(values[:, lanes], 8), upstream)]
             inner = [
                 jnp.sum(d * one, axis=0, keepdims=True) for d, one in zip(dweights, weights)
             ]
@@ -579,7 +579,7 @@
             return carry
 
         def part_of(work, i, of):
-            count = heads // 4
+            count = heads // 8
 
             def task():
                 lax.fori_loop(count * i // of, count * (i + 1) // of, work, 0)
@@ -588,7 +588,7 @@
 
         def forward_piece(i):
             def task():
-                of = heads // 4 // PIECES
+                of = heads // 8 // PIECES
                 lax.fori_loop(i * of, (i + 1) * of, forward, 0)
                 pass_piece(resid, i)()
 
@@ -606,8 +606,8 @@
         )
 
         def sort_out(i, carry):
-            lanes = pl.ds(pl.multiple_of(i * 256, 256), 256)
-            high = pl.ds(pl.multiple_of(half_width + i * 256, 256), 256)
+            lanes = pl.ds(pl.multiple_of(i * 512, 512), 512)
+            high = pl.ds(pl.multiple_of(half_width + i * 512, 512), 512)
             taken = [dkeys[:, lanes], dvalues[:, lanes], dkeys[:, high], dvalues[:, high]]
             blocks = [
                 jnp.concatenate([one[64 * c : 64 * c + 64] for one in taken], axis=0)
@@ -615,11 +615,11 @@
             ]
             blocks = [dot(perm_t[...], block).astype(BF) for block in blocks]
             gparts[:, :, :, :, lanes] = jnp.concatenate(blocks, axis=0).reshape(
-                RING, RING, 2, 2 * CAP, 256
+                RING, RING, 2, 2 * CAP, 512
             )
             return carry
 
-        lax.fori_loop(0, half_width // 256, sort_out, 0)
+        lax.fori_loop(0, half_width // 512, sort_out, 0)
 
         grad_stream = scatter(
             links, halves, gparts, grad_land, grad_base

time: 97.1 us -> 92.6 us (0.954)
  Pallas kernels: 96.3 us -> 91.3 us
    pallas_call x1, Pallas kernels: 92.8 us -> 87.9 us  [local(): pl.pallas_call(lambda *refs: kernel(sections, *refs), out_shape=(jax.Shap...]
where the time goes in v5:
time: 92.6 us; the launch traced here: 92 us
  Pallas kernels  91.3 us (99%)
    pallas_call x1, Pallas kernels, local(): pl.pallas_call(lambda *refs: kernel(sections, *refs), out_shape=(jax.Shap...  87.9 us
    pallas_call x1, Pallas kernels, local(): pl.pallas_call(place_rows, grid=(steps,), out_shape=(jax.ShapeDtypeStruct...  3.48 us

profile of v5, /device:TPU:129, one launch (start us, length us, event | category | flops | bytes accessed | tf_op | source)
XLA Modules:
  0.0 92.0 jit_solution(3582914504238875150)
XLA Ops:
  0.6 87.9 %shard_map.112 = (bf16[128,5120]{1,0:T(8,128)(2,1)}, bf16[128,5120]{1,0:T(8,128)(2,1)}, bf16[16,2560]{1,0:T(8,128)(2,1)}, bf16[16,2560]{1,0:T(8,128)(2,1)}, s32[8,128]{1,0:T(8,128)}, /*index=5*/f32[16,2560]{1,0:T(8,128)}) custom-call(bf16[4,2,5120]{2,1,0:T(2,128)(2,1)} %bitcast.14, bf16[128,5120]{1,0:T(8,128)(2,1)} %bitcast.12, bf16[128,5120]{1,0:T(8,128)(2,1)} %bitcast.13, ...), custom_call_target="tpu_custom_call" | custom-call | tf_op jit(solution)/shard_map/pallas_call | solution.py:678
  88.5 3.5 %shard_map.113 = (bf16[128,5120]{1,0:T(8,128)(2,1)}, bf16[128,5120]{1,0:T(8,128)(2,1)}, f32[4,2,5120]{2,1,0:T(2,128)}) custom-call(bf16[128,5120]{1,0:T(8,128)(2,1)} %get-tuple-element.12.base, bf16[128,5120]{1,0:T(8,128)(2,1)} %get-tuple-element.13.before, bf16[16,2560]{1,0:T(8,128)(2,1)} %get-tuple-element.14.own_rows, ...), custom_call_target="tpu_custom_call" | custom-call | tf_op jit(solution)/shard_map/pallas_call | solution.py:738

commit v6 on v5

--- a/solution.py
+++ b/solution.py
@@ -368,11 +368,11 @@
 
     def pick(source, target):
         def one(i, carry):
-            lanes = pl.ds(pl.multiple_of(i * 512, 512), 512)
+            lanes = pl.ds(pl.multiple_of(i * 1280, 1280), 1280)
             target[:, lanes] = dot(onehot, source[:, lanes]).astype(target.dtype)
             return carry
 
-        lax.fori_loop(0, width // 512, one, 0)
+        lax.fori_loop(0, width // 1280, one, 0)
 
     def fold(rows):
         return jnp.concatenate([rows[:CAP, :half_width], rows[:CAP, half_width:]], axis=0)
@@ -387,27 +387,27 @@
         hacc[...] = jnp.zeros_like(hacc)
 
         def into(k, carry):
-            lanes = pl.ds(pl.multiple_of(k * 512, 512), 512)
-            block = gcap[:, :, :, :, lanes].reshape(-1, 2 * CAP, 512).astype(F32)
-            low = block[:, :CAP].reshape(-1, 512).astype(BF)
-            high = block[:, CAP:].reshape(-1, 512).astype(BF)
-            high_lanes = pl.ds(pl.multiple_of(half_width + k * 512, 512), 512)
+            lanes = pl.ds(pl.multiple_of(k * 1280, 1280), 1280)
+            block = gcap[:, :, :, :, lanes].reshape(-1, 2 * CAP, 1280).astype(F32)
+            low = block[:, :CAP].reshape(-1, 1280).astype(BF)
+            high = block[:, CAP:].reshape(-1, 1280).astype(BF)
+            high_lanes = pl.ds(pl.multiple_of(half_width + k * 1280, 1280), 1280)
             hacc[...] += dot(win[:, lanes], low, NT) + dot(win[:, high_lanes], high, NT)
             return carry
 
-        lax.fori_loop(0, half_width // 512, into, 0)
+        lax.fori_loop(0, half_width // 1280, into, 0)
         hidden[...] = jax.nn.gelu(hacc[...]).T.astype(BF)
 
         def out(k, carry):
-            lanes = pl.ds(pl.multiple_of(k * 512, 512), 512)
-            high_lanes = pl.ds(pl.multiple_of(half_width + k * 512, 512), 512)
-            low = dot(hidden[...], wout[:, lanes]).reshape(-1, CAP, 512)
-            high = dot(hidden[...], wout[:, high_lanes]).reshape(-1, CAP, 512)
+            lanes = pl.ds(pl.multiple_of(k * 1280, 1280), 1280)
+            high_lanes = pl.ds(pl.multiple_of(half_width + k * 1280, 1280), 1280)
+            low = dot(hidden[...], wout[:, lanes]).reshape(-1, CAP, 1280)
+            high = dot(hidden[...], wout[:, high_lanes]).reshape(-1, CAP, 1280)
             block = jnp.concatenate([low, high], axis=1).astype(BF)
-            parts[:, :, :, :, lanes] = block.reshape(RING, RING, 2, 2 * CAP, 512)
+            parts[:, :, :, :, lanes] = block.reshape(RING, RING, 2, 2 * CAP, 1280)
             return carry
 
-        lax.fori_loop(0, half_width // 512, out, 0)
+        lax.fori_loop(0, half_width // 1280, out, 0)
 
     ret_land = (land_a, land_b, land_c)
     grad_land = (gland_a, gland_b, gland_c)
@@ -485,11 +485,11 @@
             loads[0].wait()
 
             def one(i, carry):
-                rows = pl.ds(pl.multiple_of(i * 16, 16), 16)
+                rows = pl.ds(pl.multiple_of(i * 32, 32), 32)
                 queries[rows, :] = scaled(cur[rows, :].astype(F32), attn_ref[...]).astype(BF)
                 return carry
 
-            lax.fori_loop(0, tokens // 16, one, 0)
+            lax.fori_loop(0, tokens // 32, one, 0)
 
         def pick_rows():
             pick(cur, picked)

time: 92.6 us -> 91.5 us (0.988)
  Pallas kernels: 91.3 us -> 89.8 us
    pallas_call x1, Pallas kernels: 87.9 us -> 86.3 us  [local(): pl.pallas_call(lambda *refs: kernel(sections, *refs), out_shape=(jax.Shap...]
where the time goes in v6:
time: 91.5 us; the launch traced here: 90.4 us
  Pallas kernels  89.8 us (98%)
    pallas_call x1, Pallas kernels, local(): pl.pallas_call(lambda *refs: kernel(sections, *refs), out_shape=(jax.Shap...  86.3 us
    pallas_call x1, Pallas kernels, local(): pl.pallas_call(place_rows, grid=(steps,), out_shape=(jax.ShapeDtypeStruct...  3.48 us

profile of v6, /device:TPU:129, one launch (start us, length us, event | category | flops | bytes accessed | tf_op | source)
XLA Modules:
  0.0 90.4 jit_solution(10142234492591513442)
XLA Ops:
  0.6 86.3 %shard_map.112 = (bf16[128,5120]{1,0:T(8,128)(2,1)}, bf16[128,5120]{1,0:T(8,128)(2,1)}, bf16[16,2560]{1,0:T(8,128)(2,1)}, bf16[16,2560]{1,0:T(8,128)(2,1)}, s32[8,128]{1,0:T(8,128)}, /*index=5*/f32[16,2560]{1,0:T(8,128)}) custom-call(bf16[4,2,5120]{2,1,0:T(2,128)(2,1)} %bitcast.14, bf16[128,5120]{1,0:T(8,128)(2,1)} %bitcast.12, bf16[128,5120]{1,0:T(8,128)(2,1)} %bitcast.13, ...), custom_call_target="tpu_custom_call" | custom-call | tf_op jit(solution)/shard_map/pallas_call | solution.py:678
  86.9 3.5 %shard_map.113 = (bf16[128,5120]{1,0:T(8,128)(2,1)}, bf16[128,5120]{1,0:T(8,128)(2,1)}, f32[4,2,5120]{2,1,0:T(2,128)}) custom-call(bf16[128,5120]{1,0:T(8,128)(2,1)} %get-tuple-element.12.base, bf16[128,5120]{1,0:T(8,128)(2,1)} %get-tuple-element.13.before, bf16[16,2560]{1,0:T(8,128)(2,1)} %get-tuple-element.14.own_rows, ...), custom_call_target="tpu_custom_call" | custom-call | tf_op jit(solution)/shard_map/pallas_call | solution.py:738
